TPU v7x, 32 devices: a whole 2x2x4 slice. The times are simulated.
32 devices in a mesh: groups: 2 (over x), pool: 16 (over z, y, core).
Axes of the slice: x: 2, y: 2, z: 4, core: 2. Of those that a mesh axis runs over, the one named last changes fastest.
Arguments:
- queries: bfloat16 [32, 1024, 2304], P(('groups', 'pool')), parts along dimension 0, may hold values from -80 to 80
- pool_cache: bfloat16 [3072, 9216], P(('groups', 'pool')), parts along dimension 0, may hold values from -5 to 5
- new_raw: bfloat16 [128, 9216], P(('groups', 'pool')), parts along dimension 0, may hold values from -700 to 700
- norm_gain: bfloat16 [512], replicated, may hold values from 0.5 to 1.5
- hit_pages: int32 [32], P('groups'), parts along dimension 0, may hold values from 36 to 48, as said below
- prompt_len: int32 [32], P('groups'), parts along dimension 0, may hold values from 592 to 832, as said below
- page_holder: int32 [32, 48], P('groups'), parts along dimension 0, may hold values from 0 to 15, as said below
- page_slot: int32 [32, 48], P('groups'), parts along dimension 0, may hold values from 0 to 95
- page_owner: int32 [32, 52, 1], P('groups'), parts along dimension 0, may hold values from 0 to 15; in each aligned block of 52 rows (0 to 51, 52 to 103, ..., all dimensions but the last counted through in order) at most 4 rows name the same one
Outputs:
- context: bfloat16 [32, 1024, 2048], P(('groups', 'pool')), parts along dimension 0
- delivered: bfloat16 [2048, 9216], P(('groups', 'pool')), parts along dimension 0
There are 2 independent parts, one for each index of `groups`. A program takes and returns all parts, laid end to end along the dimension named above; an argument that names none is the same for every part. Nothing has to cross between parts.
Inputs may be any that keep to these rules, and one draw needn't show every extreme that they name: `hit_pages`: at least three quarters of 48; 48 in some prompt. prompt_len - 16 * hit_pages lies between a quarter of 64 and 64; one prompt has both 48 hit pages and 64 miss tokens. `page_holder`: the pages of one prompt lie in runs of at most 6 consecutive pages, each run on another pool device, so no device holds more than 6 pages of one prompt. `page_owner`: among the 52 pages of one prompt no owner is named more than 4 times.
All inputs are finite; a program needn't handle non-finite values.
Results may differ from a plain program's by a relative error of at most 0.0047.
Values may be sent and summed in bfloat16 or wider, within the bound.
A program may use at most 192 MiB of HBM per device.

v0:
```python
import jax
import jax.numpy as jnp
from jax import lax
from jax.sharding import PartitionSpec as P

LATENT_WIDTH = 512
ROPE = 64
PAGE = 16
TPW = 16


score_scale = 0.07216878364870323
rope_base = 10000.0
norm_eps = 1e-06


def swapped(value, axis, stride):
    mask = 2**stride
    pairs = [(source, source ^ mask) for source in range(lax.axis_size(axis))]
    return lax.ppermute(value, axis, pairs)


def rope_tables(positions, rotary_width):
    half_width = rotary_width // 2
    frequencies = rope_base ** (jnp.arange(half_width).astype(jnp.float32) * (-2.0 / rotary_width))
    angles = positions.astype(jnp.float32)[:, None] * frequencies[None, :]
    return (jnp.cos(angles), jnp.sin(angles))


def rotate(values, cosine, sine_table):
    half_width = values.shape[-1] // 2
    lower = values[..., :half_width]
    upper = values[..., half_width:]
    return jnp.concatenate(
        [lower * cosine - upper * sine_table, upper * cosine + lower * sine_table], axis=-1
    )


def fresh_keys(raw_rows, norm_gain, hit_count, miss_count):
    latent = raw_rows[:, :LATENT_WIDTH]
    rotary = raw_rows[:, LATENT_WIDTH:]
    mean_square = jnp.mean(latent * latent, axis=1, keepdims=True)
    normed = latent * lax.rsqrt(mean_square + norm_eps) * norm_gain.astype(jnp.float32)[None, :]
    row_steps = jnp.arange(raw_rows.shape[0])
    cosine, sine_table = rope_tables(hit_count * PAGE + row_steps, ROPE)
    turned = rotate(rotary, cosine, sine_table)
    joined = jnp.concatenate([normed, turned], axis=1)
    return jnp.where((row_steps < miss_count)[:, None], joined, 0.0).astype(jnp.bfloat16)


def pick_rows(slot_position, valid_rows, rows, slot_total):
    selector = (jnp.arange(slot_total)[:, None] == slot_position[None, :]) & valid_rows[None, :]
    return jnp.dot(selector.astype(jnp.bfloat16), rows, preferred_element_type=jnp.float32).astype(
        jnp.bfloat16
    )


def turn_queries(query_rows, hits):
    batch, miss_rows = (query_rows.shape[0], query_rows.shape[1])
    row_steps = jnp.arange(miss_rows)
    positions = (hits[:, None] * PAGE + row_steps[None, :]).reshape(-1)
    cosine, sine_table = rope_tables(positions, ROPE)
    cosine = cosine.reshape(batch, miss_rows, 1, -1)
    sine_table = sine_table.reshape(batch, miss_rows, 1, -1)
    turned = rotate(query_rows[..., LATENT_WIDTH:].astype(jnp.float32), cosine, sine_table).astype(
        jnp.bfloat16
    )
    return jnp.concatenate([query_rows[..., :LATENT_WIDTH], turned], axis=3)


def attend_block(head_queries, latent_keys, hits, misses):
    row_count = head_queries.shape[1]
    key_count = latent_keys.shape[1]
    cached_rows = key_count - row_count
    row_steps = jnp.arange(row_count)
    key_steps = jnp.arange(key_count)
    cached_live = key_steps[None, :] // PAGE < hits[:, None]
    fresh_steps = key_steps - cached_rows
    fresh_live = (fresh_steps[None, None, :] <= row_steps[None, :, None]) & (
        fresh_steps[None, None, :] < misses[:, None, None]
    )
    allowed = jnp.where(
        (key_steps < cached_rows)[None, None, :], cached_live[:, None, :], fresh_live
    )
    scores = (
        jnp.einsum("lgqu,ltu->lqgt", head_queries, latent_keys, preferred_element_type=jnp.float32)
        * score_scale
    )
    scores = jnp.where(allowed[:, None, :, :], scores, -jnp.inf)
    row_max = jnp.max(scores, axis=3, keepdims=True)
    weights = jnp.exp(scores - row_max)
    attention_weights = (weights / jnp.sum(weights, axis=3, keepdims=True)).astype(jnp.bfloat16)
    context = jnp.einsum(
        "rylp,rpj->rlyj",
        attention_weights,
        latent_keys[:, :, :LATENT_WIDTH],
        preferred_element_type=jnp.float32,
    )
    return jnp.where((row_steps[None, :] < misses[:, None])[:, :, None, None], context, 0.0)


def shards(
    queries,
    pool_cache,
    new_raw,
    norm_gain,
    hit_pages,
    prompt_len,
    page_holder,
    page_slot,
    page_owner,
):
    pool_size = lax.axis_size("pool")
    device_index = lax.axis_index("pool")
    pages_max = page_holder.shape[1]
    slot_cap = max(2, 2 * pages_max // pool_size)
    features = pool_cache.shape[1] // PAGE
    misses = prompt_len - PAGE * hit_pages
    page_steps = jnp.arange(pages_max)
    page_live = page_steps[None, :] < hit_pages[:, None]
    held_here = page_live & (page_holder == device_index)
    held_rank = jnp.cumsum(held_here.astype(jnp.int32), axis=1) - 1
    cap_steps = jnp.arange(slot_cap)
    chosen = held_here[:, None, :] & (held_rank[:, None, :] == cap_steps[None, :, None])
    slot_index = jnp.sum(jnp.where(chosen, page_slot[:, None, :], 0), axis=2).reshape(-1)
    filled = jnp.any(chosen, axis=2).reshape(-1, 1)
    outbox = jnp.where(filled, pool_cache[slot_index], jnp.zeros((), pool_cache.dtype))
    arrived = lax.all_to_all(outbox, "pool", split_axis=0, concat_axis=0, tiled=True)
    own_hit = hit_pages[device_index]
    own_miss = misses[device_index]
    own_holder = page_holder[device_index]
    own_owner = page_owner[device_index, :, 0]
    own_live = page_steps < own_hit
    before = (
        (page_steps[None, :] < page_steps[:, None])
        & (own_holder[None, :] == own_holder[:, None])
        & own_live[None, :]
    )
    page_rank = jnp.sum(before.astype(jnp.int32), axis=1)
    source = jnp.where(own_live, own_holder * slot_cap + page_rank, 0)
    cached_pages = arrived[source]
    new_rows = new_raw.shape[0] * PAGE
    new_keys = fresh_keys(
        new_raw.astype(jnp.float32).reshape(new_rows, features), norm_gain, own_hit, own_miss
    )
    new_pages = new_keys.reshape(-1, PAGE * features)
    per_prompt = new_pages.shape[0]
    total = pages_max + per_prompt
    push_cap = max(2, (total + pool_size - 1) // pool_size)
    slot_total = pool_size * push_cap
    new_steps = jnp.arange(per_prompt)
    fresh_live = new_steps * PAGE < own_miss
    all_live = jnp.concatenate([own_live, fresh_live], axis=0)
    all_steps = jnp.arange(total)
    same_owner = (
        (all_steps[None, :] < all_steps[:, None])
        & (own_owner[None, :] == own_owner[:, None])
        & all_live[None, :]
    )
    slot_position = own_owner * push_cap + jnp.sum(same_owner.astype(jnp.int32), axis=1)
    every_page = jnp.concatenate([cached_pages, new_pages], axis=0)
    outgoing = pick_rows(slot_position, all_live, every_page, slot_total)
    delivered = lax.all_to_all(outgoing, "pool", split_axis=0, concat_axis=0, tiled=True)
    own_keys = jnp.concatenate([cached_pages.reshape(pages_max * PAGE, features), new_keys], axis=0)
    member = device_index % TPW
    group_base = device_index - member
    group_hits = lax.dynamic_slice_in_dim(hit_pages, group_base, TPW)
    group_misses = lax.dynamic_slice_in_dim(misses, group_base, TPW)
    head_dev = queries.shape[2] // features
    query_rows = queries.reshape(TPW, -1, head_dev, features)
    miss_rows = query_rows.shape[1]
    head_queries = turn_queries(query_rows, group_hits)
    block = own_keys[None]
    for bit in range(TPW.bit_length() - 1):
        other = swapped(block, "pool", bit)
        upper = member // (1 << bit) % 2 == 1
        block = jnp.where(
            upper, jnp.concatenate([other, block], axis=0), jnp.concatenate([block, other], axis=0)
        )
    context = attend_block(head_queries, block, group_hits, group_misses).astype(jnp.bfloat16)
    return (context.reshape(1, TPW * miss_rows, head_dev * LATENT_WIDTH), delivered)


def solution(mesh):
    in_specs = (
        P(("groups", "pool"), None, None),
        P(("groups", "pool"), None),
        P(("groups", "pool"), None),
        P(),
        P("groups"),
        P("groups"),
        P("groups", None),
        P("groups", None),
        P("groups", None, None),
    )
    out_specs = (P(("groups", "pool"), None, None), P(("groups", "pool"), None))
    return jax.shard_map(shards, mesh=mesh, in_specs=in_specs, out_specs=out_specs, check_vma=False)
```

profile of v0, /device:TPU:1, one launch (start us, length us, event | category | flops | bytes accessed | tf_op | source)
XLA Modules:
  0.0 748.3 jit_solution(13517405048344921595)
XLA Ops:
  0.7 0.9 fusion.46
  1.6 0.2 reduce_window_sum.11
  1.8 0.2 fusion.19
  1.9 0.9 select_reduce_fusion
  3.0 1.6 gather_fusion
  4.7 1.7 gather.9
  6.6 3.4 broadcast_select_fusion
  10.0 7.4 all-to-all-start
  17.3 0.6 dynamic_slice.14
  18.6 0.1 reshape.353
  18.7 0.6 dynamic_slice.16
  19.4 0.6 iota_compare_fusion.9
  20.0 0.7 fusion.41
  20.8 0.6 iota_compare_fusion.8
  21.4 0.2 convert_reduce_fusion.1
  21.6 1.4 fusion.39
  23.1 0.2 fusion.24
  23.4 40.0 %all-to-all-done = bf16[16,6,9216]{2,1,0:T(8,128)(2,1)} async-done(((bf16[16,6,9216]{2,1,0:T(8,128)(2,1)}), bf16[16,6,9216]{2,1,0:T(8,128)(2,1)}, u32[]{:S(2)}, u32[]{:S(2)}) %all-to-all-start) | async-done | bytes 1769504 | tf_op jit(solution)/shard_map/all_to_all | solution.py:128
  63.5 2.0 all_to_all.15
  65.5 1.1 gather_fusion.1
  66.6 1.8 reshape.347
  68.3 1.3 maximum_bitcast_fusion
  69.6 1.6 copy.34
  71.3 3.0 collective-permute-done
  74.2 2.3 copy.35
  76.5 3.5 maximum_select_fusion.3
  80.0 4.2 copy.37
  84.2 3.4 collective-permute-start.1
  87.7 45.5 %collective-permute-done.1 = bf16[2,832,576]{1,2,0:T(8,128)(2,1)} collective-permute-done((bf16[2,832,576]{1,2,0:T(8,128)(2,1)}, bf16[2,832,576]{1,2,0:T(8,128)(2,1)}, u32[]{:S(2)}, u32[]{:S(2)}) %collective-permute-start.1) | collective-permute-done | bytes 1916960 | tf_op jit(solution)/shard_map/ppermute | solution.py:20
  133.2 4.2 copy.38
  137.4 5.4 maximum_select_fusion.2
  142.8 7.0 copy.40
  149.7 6.1 collective-permute-start.2
  155.9 89.2 %collective-permute-done.2 = bf16[4,832,576]{1,2,0:T(8,128)(2,1)} collective-permute-done((bf16[4,832,576]{1,2,0:T(8,128)(2,1)}, bf16[4,832,576]{1,2,0:T(8,128)(2,1)}, u32[]{:S(2)}, u32[]{:S(2)}) %collective-permute-start.2) | collective-permute-done | bytes 3833888 | tf_op jit(solution)/shard_map/ppermute | solution.py:20
  245.1 7.0 copy.41
  252.1 9.7 %maximum_select_fusion.1 = bf16[8,832,576]{2,1,0:T(8,128)(2,1)} fusion(bf16[4,832,576]{2,1,0:T(8,128)(2,1)} %maximum_select_fusion.2, bf16[4,832,576]{2,1,0:T(8,128)(2,1)} %copy.41, pred[]{:T(512)S(6)} %eq.79), kind=kLoop, calls=%fused_computation.13 | loop fusion | flops 11501568 | bytes 15335425 | tf_op jit(solution)/shard_map/jit(_where)/select_n | solution.py:177
  261.8 12.5 %copy.43 = bf16[8,832,576]{1,2,0:T(8,128)(2,1)} copy(bf16[8,832,576]{2,1,0:T(8,128)(2,1)} %maximum_select_fusion.1) | data formatting | bytes 15335424 | tf_op jit(solution)/shard_map/jit(_where)/select_n | solution.py:177
  274.2 1.5 collective-permute-start.3
  275.7 11.5 %reshape.350 = bf16[16,64,4,576]{3,2,1,0:T(4,128)(2,1)} reshape(bf16[1,1024,2304]{2,1,0:T(8,128)(2,1)} %param.9) | data formatting | bytes 9437184 | tf_op jit(solution)/shard_map/reshape | solution.py:170
  287.2 5.7 slice.43
  293.0 5.5 copy.54
  298.4 0.1 concatenate.56
  298.6 0.7 add_compare_fusion
  299.4 0.1 broadcast_in_dim.144
  299.5 0.6 multiply_compare_fusion
  300.2 0.7 dynamic-slice_bitcast_fusion
  300.9 0.2 convert_reduce_fusion
  301.1 0.7 multiply_add_fusion
  301.8 1.5 convolution_convert_fusion
  303.3 2.3 all_to_all.16
  305.6 6.0 all-to-all-start.1
  311.9 1.9 multiply_cosine_fusion
  313.8 0.3 copy_convert_fusion
  314.1 1.5 and_select_fusion
  315.6 1.9 subtract_convert_fusion
  317.5 336.3 %all-to-all-done.1 = bf16[16,4,9216]{2,1,0:T(4,128)(2,1)S(1)} async-done(((bf16[16,4,9216]{2,1,0:T(4,128)(2,1)}), bf16[16,4,9216]{2,1,0:T(4,128)(2,1)S(1)}, u32[]{:S(2)}, u32[]{:S(2)}) %all-to-all-start.1) | async-done | bytes 1179680 | tf_op jit(solution)/shard_map/all_to_all | solution.py:163
  653.7 1.1 all_to_all.18
  654.9 12.5 %copy.44 = bf16[8,832,576]{2,1,0:T(8,128)(2,1)} copy(bf16[8,832,576]{1,2,0:T(8,128)(2,1)} %collective-permute-done.3) | data formatting | bytes 15335424 | tf_op jit(solution)/shard_map/ppermute | solution.py:20
  667.4 18.6 %maximum_select_fusion = bf16[16,832,576]{2,1,0:T(8,128)(2,1)} fusion(bf16[8,832,576]{2,1,0:T(8,128)(2,1)} %maximum_select_fusion.1, bf16[8,832,576]{2,1,0:T(8,128)(2,1)} %copy.44, pred[]{:T(512)S(6)} %eq.78), kind=kLoop, calls=%fused_computation.3 | loop fusion | flops 23003136 | bytes 30670848 | tf_op jit(solution)/shard_map/jit(_where)/select_n | solution.py:177
  686.0 14.0 %fusion.1 = f32[16,832,64,4]{1,2,3,0:T(8,128)} fusion(bf16[16,832,576]{2,1,0:T(8,128)(2,1)} %maximum_select_fusion, bf16[16,64,4,32]{3,1,2,0:T(8,128)(2,1)S(1)} %copy-done.2, bf16[16,64,4,32]{3,1,2,0:T(8,128)(2,1)S(1)} %get-tuple-element.6, bf16[16,64,4,512]{3,1,2,0:T(8,128)(2,1)} %copy.54), kind=kOutput, calls=%fused_computation.4 | convolution fusion | flops 3940024320 | bytes 33685504 | tf_op jit(solution)/shard_map/lgqu,ltu->lqgt/dot_general | solution.py:86
  700.0 19.0 %fusion.48 = (f32[16,4,64]{2,1,0:T(4,128)S(1)}, f32[16,4,64,832]{3,2,1,0:T(8,128)}) fusion(f32[16,832,64,4]{1,2,3,0:T(8,128)} %fusion.1, pred[16,64,832]{2,1,0:T(8,128)(4,1)} %and_select_fusion), kind=kOutput, calls=%fused_computation.111 | output fusion | flops 20448064 | bytes 28131328 | tf_op jit(solution)/shard_map/sub | solution.py:91
  719.0 13.7 %fusion.14 = bf16[16,64,4,512]{3,1,2,0:T(8,128)(2,1)} fusion(pred[16,64]{1,0:T(8,128)(4,1)S(1)} %iota_compare_fusion.6, f32[16,4,64,832]{3,2,1,0:T(8,128)} %get-tuple-element.15, f32[16,4,64]{2,1,0:T(4,128)S(1)} %get-tuple-element.14, bf16[16,832,576]{2,1,0:T(8,128)(2,1)} %maximum_select_fusion), kind=kOutput, calls=%fused_computation.25 | convolution fusion | flops 3500670976 | bytes 32523264 | tf_op jit(solution)/shard_map/rylp,rpj->rlyj/dot_general | solution.py:93
  732.8 7.8 %copy.49 = bf16[16,64,4,512]{3,2,1,0:T(4,128)(2,1)} copy(bf16[16,64,4,512]{3,1,2,0:T(8,128)(2,1)} %fusion.14) | data formatting | bytes 8388608 | tf_op jit(solution)/shard_map/convert_element_type | solution.py:180
  740.5 7.7 %reshape.351 = bf16[1,1024,2048]{2,1,0:T(8,128)(2,1)} reshape(bf16[16,64,4,512]{3,2,1,0:T(4,128)(2,1)} %copy.49) | data formatting | bytes 8388608 | tf_op jit(solution)/shard_map/reshape | solution.py:181
  (43 shorter events, 1.2 us)
Async XLA Ops:
  0.6 2.4 copy-start
  6.5 10.8 %copy-start.4 = (s32[16]{0:T(128)S(1)}, s32[16]{0:T(128)}, u32[]{:S(2)}) copy-start(s32[16]{0:T(128)} %param.13) | copy-start | bytes 196
  6.6 12.0 %copy-start.3 = (bf16[4,9216]{1,0:T(4,128)(2,1)S(1)}, bf16[4,9216]{1,0:T(4,128)(2,1)}, u32[]{:S(2)}) copy-start(bf16[4,9216]{1,0:T(4,128)(2,1)} %param.11) | copy-start | bytes 221188
  6.6 12.2 %copy-start.6 = (s32[16]{0:T(128)S(1)}, s32[16]{0:T(128)}, u32[]{:S(2)}) copy-start(s32[16]{0:T(128)} %param.14) | copy-start | bytes 196
  6.6 12.8 %copy-start.5 = (bf16[512]{0:T(512)(128)(2,1)S(1)}, bf16[512]{0:T(512)(128)(2,1)}, u32[]{:S(2)}) copy-start(bf16[512]{0:T(512)(128)(2,1)} %param.12) | copy-start | bytes 3076
  10.0 53.5 %all-to-all-start = ((bf16[16,6,9216]{2,1,0:T(8,128)(2,1)}), bf16[16,6,9216]{2,1,0:T(8,128)(2,1)}, u32[]{:S(2)}, u32[]{:S(2)}) async-start(bf16[16,6,9216]{2,1,0:T(8,128)(2,1)} %broadcast_select_fusion), calls=%async_computation | async-start | bytes 4718592 | tf_op jit(solution)/shard_map/all_to_all | solution.py:128
  71.3 3.0 collective-permute-start
  84.2 48.9 %collective-permute-start.1 = (bf16[2,832,576]{1,2,0:T(8,128)(2,1)}, bf16[2,832,576]{1,2,0:T(8,128)(2,1)}, u32[]{:S(2)}, u32[]{:S(2)}) collective-permute-start(bf16[2,832,576]{1,2,0:T(8,128)(2,1)} %copy.37), channel_id=1, source_target_pairs={{0,2},{1,3},{2,0},{3,1},{4,6},{5,7},{6,4},{7,5},{8,10},{9,11},{10,... | collective-permute-start | bytes 5750792 | tf_op jit(solution)/shard_map/ppermute | solution.py:20
  149.7 95.3 %collective-permute-start.2 = (bf16[4,832,576]{1,2,0:T(8,128)(2,1)}, bf16[4,832,576]{1,2,0:T(8,128)(2,1)}, u32[]{:S(2)}, u32[]{:S(2)}) collective-permute-start(bf16[4,832,576]{1,2,0:T(8,128)(2,1)} %copy.40), channel_id=1, source_target_pairs={{0,4},{1,5},{2,6},{3,7},{4,0},{5,1},{6,2},{7,3},{8,12},{9,13},{10,... | collective-permute-start | bytes 11501576 | tf_op jit(solution)/shard_map/ppermute | solution.py:20
  274.2 380.7 %collective-permute-start.3 = (bf16[8,832,576]{1,2,0:T(8,128)(2,1)}, bf16[8,832,576]{1,2,0:T(8,128)(2,1)}, u32[]{:S(2)}, u32[]{:S(2)}) collective-permute-start(bf16[8,832,576]{1,2,0:T(8,128)(2,1)} %copy.43), channel_id=1, source_target_pairs={{0,8},{1,9},{2,10},{3,11},{4,12},{5,13},{6,14},{7,15},{8,0},{9,1},... | collective-permute-start | bytes 23003144 | tf_op jit(solution)/shard_map/ppermute | solution.py:20
  298.4 15.4 %slice-start = ((bf16[16,64,4,576]{3,2,1,0:T(4,128)(2,1)}), bf16[16,64,4,64]{3,2,1,0:T(4,128)(2,1)S(1)}, s32[]{:S(2)}) async-start(bf16[16,64,4,576]{3,2,1,0:T(4,128)(2,1)} %reshape.350), calls=%async_computation.2 | async-start | bytes 2097152 | tf_op jit(solution)/shard_map/slice | solution.py:65
  305.6 348.1 %all-to-all-start.1 = ((bf16[16,4,9216]{2,1,0:T(4,128)(2,1)}), bf16[16,4,9216]{2,1,0:T(4,128)(2,1)S(1)}, u32[]{:S(2)}, u32[]{:S(2)}) async-start(bf16[16,4,9216]{2,1,0:T(4,128)(2,1)} %all_to_all.16), calls=%async_computation.1 | async-start | bytes 2359296 | tf_op jit(solution)/shard_map/all_to_all | solution.py:163
  667.4 18.6 %copy-start.2 = (bf16[16,64,4,32]{3,1,2,0:T(8,128)(2,1)S(1)}, bf16[16,64,4,32]{3,1,2,0:T(8,128)(2,1)}, u32[]{:S(2)}) copy-start(bf16[16,64,4,32]{3,1,2,0:T(8,128)(2,1)} %get-tuple-element.7) | copy-start | bytes 786436
  732.8 15.5 %copy-start.1 = (bf16[96,9216]{1,0:T(8,128)(2,1)S(1)}, bf16[96,9216]{1,0:T(8,128)(2,1)}, u32[]{:S(2)}) copy-start(bf16[96,9216]{1,0:T(8,128)(2,1)} %param.10) | copy-start | bytes 5308420
where the time goes:
time: 752 us; the launch traced here: 748 us
  waiting for transfers between devices  514 us (68%)
  local copies, waits for them, and re-layouts  105 us (14%)
  other arithmetic  74.4 us (10%)
  matrix products  29.3 us (4%)
  starting transfers between devices  24.5 us (3%)
    all_to_all x1, waiting for transfers between devices, shards(): lax.all_to_all(outgoing, 'pool', split_axis=0, concat_axis=0, tiled=True)  336 us
    ppermute x4, waiting for transfers between devices, swapped(): return lax.ppermute(value, axis, pairs)  138 us
    all_to_all x1, waiting for transfers between devices, shards(): lax.all_to_all(outbox, 'pool', split_axis=0, concat_axis=0, tiled=True)  40 us
    select_n x4, other arithmetic, shards(): jnp.where(upper, jnp.concatenate([other, block], axis=0), jnp.concatenate...  37.1 us
    ppermute x4, local copies, waits for them, and re-layouts, swapped(): return lax.ppermute(value, axis, pairs)  26 us
    select_n x3, local copies, waits for them, and re-layouts, shards(): jnp.where(upper, jnp.concatenate([other, block], axis=0), jnp.concatenate...  23.7 us
    sub x1, other arithmetic, attend_block(): weights = jnp.exp(scores - row_max)  19 us
  transfers between devices with their start and end apart: 6, of which 5 were waited for; matrix products, arithmetic and copies ran while one was open for 5% of the time, Pallas kernels for 0%

commit v1 on v0

--- a/solution.py
+++ b/solution.py
@@ -1,23 +1,23 @@
+import functools
+
 import jax
 import jax.numpy as jnp
 from jax import lax
+from jax.experimental import pallas as pl
+from jax.experimental.pallas import tpu as pltpu
 from jax.sharding import PartitionSpec as P
 
 LATENT_WIDTH = 512
 ROPE = 64
 PAGE = 16
 TPW = 16
+PACK = 128
+MESH = pl.DeviceIdType.MESH
 
 
 score_scale = 0.07216878364870323
 rope_base = 10000.0
 norm_eps = 1e-06
-
-
-def swapped(value, axis, stride):
-    mask = 2**stride
-    pairs = [(source, source ^ mask) for source in range(lax.axis_size(axis))]
-    return lax.ppermute(value, axis, pairs)
 
 
 def rope_tables(positions, rotary_width):
@@ -65,38 +65,232 @@
     turned = rotate(query_rows[..., LATENT_WIDTH:].astype(jnp.float32), cosine, sine_table).astype(
         jnp.bfloat16
     )
-    return jnp.concatenate([query_rows[..., :LATENT_WIDTH], turned], axis=3)
-
-
-def attend_block(head_queries, latent_keys, hits, misses):
-    row_count = head_queries.shape[1]
-    key_count = latent_keys.shape[1]
-    cached_rows = key_count - row_count
-    row_steps = jnp.arange(row_count)
-    key_steps = jnp.arange(key_count)
-    cached_live = key_steps[None, :] // PAGE < hits[:, None]
-    fresh_steps = key_steps - cached_rows
-    fresh_live = (fresh_steps[None, None, :] <= row_steps[None, :, None]) & (
-        fresh_steps[None, None, :] < misses[:, None, None]
-    )
-    allowed = jnp.where(
-        (key_steps < cached_rows)[None, None, :], cached_live[:, None, :], fresh_live
-    )
-    scores = (
-        jnp.einsum("lgqu,ltu->lqgt", head_queries, latent_keys, preferred_element_type=jnp.float32)
-        * score_scale
-    )
-    scores = jnp.where(allowed[:, None, :, :], scores, -jnp.inf)
-    row_max = jnp.max(scores, axis=3, keepdims=True)
+    by_head = lambda value: value.transpose(0, 2, 1, 3).reshape(batch, -1, value.shape[-1])
+    latent = by_head(query_rows[..., :LATENT_WIDTH])
+    rotary = by_head(turned)
+    blank = jnp.zeros_like(rotary)
+    paired = jnp.concatenate(
+        [jnp.concatenate([rotary, blank], axis=2), jnp.concatenate([blank, rotary], axis=2)], axis=1
+    )
+    return latent, paired
+
+
+def pack_keys(keys):
+    rotary = keys[:, LATENT_WIDTH:]
+    spare = PACK * (LATENT_WIDTH // ROPE) - keys.shape[0]
+    rotary = jnp.concatenate([rotary, jnp.zeros((spare, ROPE), keys.dtype)], axis=0)
+    packed = rotary.reshape(-1, PACK, ROPE).transpose(1, 0, 2).reshape(PACK, LATENT_WIDTH)
+    return jnp.concatenate([keys[:, :LATENT_WIDTH], packed], axis=0)
+
+
+def gather_body(own, out, local_sem, up_sem, down_sem, y_sem, core_sem, recv_sem):
+    me = lax.axis_index("pool")
+    member = lax.rem(me, TPW)
+    base = me - member
+    z, y, c = member // 4, lax.rem(member // 2, 2), lax.rem(member, 2)
+
+    def slot_of(zz, yy, cc):
+        return zz * 4 + yy * 2 + cc
+
+    across = base + slot_of(z, 1 - y, c)
+    twin = base + slot_of(z, y, 1 - c)
+    above = base + slot_of(lax.rem(z + 1, 4), y, c)
+    below = base + slot_of(lax.rem(z + 3, 4), y, c)
+    has_up, has_down = z < 3, z > 0
+
+    barrier = pltpu.get_barrier_semaphore()
+    pl.semaphore_signal(barrier, inc=1, device_id={"pool": across}, device_id_type=MESH)
+    pl.semaphore_signal(barrier, inc=1, device_id={"pool": twin}, device_id_type=MESH)
+
+    @pl.when(has_up)
+    def _():
+        pl.semaphore_signal(barrier, inc=1, device_id={"pool": above}, device_id_type=MESH)
+
+    @pl.when(has_down)
+    def _():
+        pl.semaphore_signal(barrier, inc=1, device_id={"pool": below}, device_id_type=MESH)
+
+    pl.semaphore_wait(barrier, 2 + has_up.astype(jnp.int32) + has_down.astype(jnp.int32))
+
+    def copy(zz, yy, cc, sem, device, first):
+        slot = slot_of(zz, yy, cc)
+        return pltpu.make_async_remote_copy(
+            src_ref=own if first else out.at[slot],
+            dst_ref=out.at[slot],
+            send_sem=sem,
+            recv_sem=recv_sem.at[slot],
+            device_id={"pool": device},
+            device_id_type=MESH,
+        )
+
+    def arrive(zz, yy, cc):
+        copy(zz, yy, cc, core_sem.at[0], twin, False).wait_recv()
+
+    def column(zz, act, up, down, first=False):
+        if up:
+            @pl.when(has_up)
+            def _():
+                act(copy(zz, y, c, up_sem.at[zz], above, first))
+        if down:
+            @pl.when(has_down)
+            def _():
+                act(copy(zz, y, c, down_sem.at[zz], below, first))
+        act(copy(zz, y, c, y_sem.at[zz], across, first))
+        act(copy(zz, y, c, core_sem.at[zz * 2 + y], twin, first))
+
+    def side(zz):
+        arrive(zz, 1 - y, c)
+        copy(zz, 1 - y, c, core_sem.at[zz * 2 + 1 - y], twin, False).start()
+
+    def sides(step):
+        @pl.when(z >= step)
+        def _():
+            side(z - step)
+        if step:
+            @pl.when(z + step <= 3)
+            def _():
+                side(z + step)
+
+    start = lambda item: item.start()
+    mine = pltpu.make_async_copy(own, out.at[member], local_sem)
+    mine.start()
+    column(z, start, True, True, True)
+    for step in range(1, 4):
+        @pl.when(z >= step)
+        def _():
+            arrive(z - step, y, c)
+            column(z - step, start, True, False)
+
+        @pl.when(z + step <= 3)
+        def _():
+            arrive(z + step, y, c)
+            column(z + step, start, False, True)
+
+        sides(step - 1)
+    sides(3)
+    for zz in range(4):
+        for yy in range(2):
+            arrive(zz, yy, 1 - c)
+    ended = lambda item: item.wait_send()
+    mine.wait()
+    column(z, ended, True, True, True)
+    copy(z, 1 - y, c, core_sem.at[z * 2 + 1 - y], twin, False).wait_send()
+    for step in range(1, 4):
+        @pl.when(z >= step)
+        def _():
+            column(z - step, ended, True, False)
+            copy(z - step, 1 - y, c, core_sem.at[(z - step) * 2 + 1 - y], twin, False).wait_send()
+
+        @pl.when(z + step <= 3)
+        def _():
+            column(z + step, ended, False, True)
+            copy(z + step, 1 - y, c, core_sem.at[(z + step) * 2 + 1 - y], twin, False).wait_send()
+
+
+def gather_keys(own):
+    return pl.pallas_call(
+        gather_body,
+        out_shape=jax.ShapeDtypeStruct((TPW,) + own.shape, own.dtype),
+        in_specs=[pl.BlockSpec(memory_space=pl.ANY)],
+        out_specs=pl.BlockSpec(memory_space=pl.ANY),
+        scratch_shapes=[
+            pltpu.SemaphoreType.DMA,
+            pltpu.SemaphoreType.DMA((4,)),
+            pltpu.SemaphoreType.DMA((4,)),
+            pltpu.SemaphoreType.DMA((4,)),
+            pltpu.SemaphoreType.DMA((8,)),
+            pltpu.SemaphoreType.DMA((TPW,)),
+        ],
+        compiler_params=pltpu.CompilerParams(collective_id=0, has_side_effects=True),
+    )(own)
+
+
+def attend_one(latent_queries, paired_queries, keys, hits, misses, key_count, miss_rows):
+    rows = latent_queries.shape[0]
+    cached_rows = key_count - miss_rows
+    contract = (((1,), (1,)), ((), ()))
+    latent_keys = keys[:key_count, :]
+    scores = lax.dot_general(
+        latent_queries, latent_keys, contract, preferred_element_type=jnp.float32
+    )
+    parts = []
+    for pair in range(LATENT_WIDTH // 128):
+        if pair * 2 * PACK >= key_count:
+            break
+        both = lax.dot_general(
+            paired_queries,
+            keys[key_count:, pair * 128 : (pair + 1) * 128],
+            contract,
+            preferred_element_type=jnp.float32,
+        )
+        parts += [both[:rows], both[rows:]]
+    rotary = jnp.concatenate(parts, axis=1)[:, :key_count]
+    scores = (scores + rotary) * score_scale
+    row_steps = lax.rem(lax.broadcasted_iota(jnp.int32, (rows, 1), 0), miss_rows)
+    key_steps = lax.broadcasted_iota(jnp.int32, (rows, key_count), 1)
+    fresh_end = cached_rows + jnp.minimum(row_steps + 1, misses)
+    allowed = (key_steps < hits * PAGE) | ((key_steps >= cached_rows) & (key_steps < fresh_end))
+    scores = jnp.where(allowed, scores, -jnp.inf)
+    row_max = jnp.max(scores, axis=1, keepdims=True)
     weights = jnp.exp(scores - row_max)
-    attention_weights = (weights / jnp.sum(weights, axis=3, keepdims=True)).astype(jnp.bfloat16)
-    context = jnp.einsum(
-        "rylp,rpj->rlyj",
-        attention_weights,
-        latent_keys[:, :, :LATENT_WIDTH],
-        preferred_element_type=jnp.float32,
-    )
-    return jnp.where((row_steps[None, :] < misses[:, None])[:, :, None, None], context, 0.0)
+    total = jnp.sum(weights, axis=1, keepdims=True)
+    context = jnp.dot(
+        weights.astype(jnp.bfloat16), latent_keys, preferred_element_type=jnp.float32
+    )
+    return jnp.where(row_steps < misses, context / total, 0.0)
+
+
+def attend_body(key_count, miss_rows, hits, misses, picks, lq, pq, keys, context, pages):
+    prompt = pl.program_id(0)
+    result = attend_one(
+        lq[0], pq[0], keys.at[0], hits[prompt], misses[prompt], key_count, miss_rows
+    ).astype(context.dtype)
+    for head in range(result.shape[0] // miss_rows):
+        context[:, head * LATENT_WIDTH : (head + 1) * LATENT_WIDTH] = result[
+            head * miss_rows : (head + 1) * miss_rows
+        ]
+    slots = pages.shape[1]
+    for rank in range(slots):
+        page = picks[prompt * slots + rank]
+        live = page >= 0
+        page = jnp.maximum(page, 0)
+        latent = keys[0, pl.ds(pl.multiple_of(page * PAGE, PAGE), PAGE), :]
+        place = pl.multiple_of(key_count + lax.rem(page, PACK // PAGE) * PAGE, PAGE)
+        packed = keys[0, pl.ds(place, PAGE), :]
+        part = page // (PACK // PAGE)
+        rotary = packed[:, :ROPE]
+        for index in range(1, LATENT_WIDTH // ROPE):
+            rotary = jnp.where(part == index, packed[:, index * ROPE : (index + 1) * ROPE], rotary)
+        pages[0, rank, :, :LATENT_WIDTH] = jnp.where(live, latent, jnp.zeros_like(latent))
+        pages[0, rank, :, LATENT_WIDTH:] = jnp.where(live, rotary, jnp.zeros_like(rotary))
+
+
+def attend(latent_queries, paired_queries, keys, hits, misses, picks, key_count, miss_rows):
+    prompts, rows, _ = latent_queries.shape
+    heads = rows // miss_rows
+    slots = picks.shape[1]
+    whole = lambda shape: pl.BlockSpec((1,) + shape, lambda p, *_: (p,) + (0,) * len(shape))
+    return pl.pallas_call(
+        functools.partial(attend_body, key_count, miss_rows),
+        grid_spec=pltpu.PrefetchScalarGridSpec(
+            num_scalar_prefetch=3,
+            grid=(prompts,),
+            in_specs=[
+                whole(latent_queries.shape[1:]),
+                whole(paired_queries.shape[1:]),
+                whole(keys.shape[1:]),
+            ],
+            out_specs=[
+                pl.BlockSpec((miss_rows, heads * LATENT_WIDTH), lambda p, *_: (p, 0)),
+                whole((slots, PAGE, LATENT_WIDTH + ROPE)),
+            ],
+        ),
+        out_shape=[
+            jax.ShapeDtypeStruct((prompts * miss_rows, heads * LATENT_WIDTH), jnp.bfloat16),
+            jax.ShapeDtypeStruct((prompts, slots, PAGE, LATENT_WIDTH + ROPE), jnp.bfloat16),
+        ],
+        compiler_params=pltpu.CompilerParams(vmem_limit_bytes=40 * 1024 * 1024),
+    )(hits, misses, picks.reshape(-1), latent_queries, paired_queries, keys)
 
 
 def shards(
@@ -149,18 +343,6 @@
     push_cap = max(2, (total + pool_size - 1) // pool_size)
     slot_total = pool_size * push_cap
     new_steps = jnp.arange(per_prompt)
-    fresh_live = new_steps * PAGE < own_miss
-    all_live = jnp.concatenate([own_live, fresh_live], axis=0)
-    all_steps = jnp.arange(total)
-    same_owner = (
-        (all_steps[None, :] < all_steps[:, None])
-        & (own_owner[None, :] == own_owner[:, None])
-        & all_live[None, :]
-    )
-    slot_position = own_owner * push_cap + jnp.sum(same_owner.astype(jnp.int32), axis=1)
-    every_page = jnp.concatenate([cached_pages, new_pages], axis=0)
-    outgoing = pick_rows(slot_position, all_live, every_page, slot_total)
-    delivered = lax.all_to_all(outgoing, "pool", split_axis=0, concat_axis=0, tiled=True)
     own_keys = jnp.concatenate([cached_pages.reshape(pages_max * PAGE, features), new_keys], axis=0)
     member = device_index % TPW
     group_base = device_index - member
@@ -169,16 +351,41 @@
     head_dev = queries.shape[2] // features
     query_rows = queries.reshape(TPW, -1, head_dev, features)
     miss_rows = query_rows.shape[1]
-    head_queries = turn_queries(query_rows, group_hits)
-    block = own_keys[None]
-    for bit in range(TPW.bit_length() - 1):
-        other = swapped(block, "pool", bit)
-        upper = member // (1 << bit) % 2 == 1
-        block = jnp.where(
-            upper, jnp.concatenate([other, block], axis=0), jnp.concatenate([block, other], axis=0)
+    latent_queries, paired_queries = turn_queries(query_rows, group_hits)
+    keys = gather_keys(pack_keys(own_keys))
+    group_owner = lax.dynamic_slice_in_dim(page_owner[:, :, 0], group_base, TPW)
+    group_live = jnp.concatenate(
+        [page_steps < group_hits[:, None], new_steps * PAGE < group_misses[:, None]], axis=1
+    )
+    taken = group_live & (group_owner == device_index)
+    rank = jnp.cumsum(taken.astype(jnp.int32), axis=1) - 1
+    all_steps = jnp.arange(total)
+    hit = taken[:, None, :] & (rank[:, None, :] == jnp.arange(push_cap)[None, :, None])
+    picks = jnp.sum(jnp.where(hit, all_steps + 1, 0), axis=2) - 1
+    context, pages = attend(
+        latent_queries,
+        paired_queries,
+        keys,
+        group_hits,
+        group_misses,
+        picks,
+        own_keys.shape[0],
+        miss_rows,
+    )
+    if pool_size == TPW:
+        delivered = pages.reshape(slot_total, PAGE * features)
+    else:
+        all_live = jnp.concatenate([own_live, new_steps * PAGE < own_miss], axis=0)
+        same_owner = (
+            (all_steps[None, :] < all_steps[:, None])
+            & (own_owner[None, :] == own_owner[:, None])
+            & all_live[None, :]
         )
-    context = attend_block(head_queries, block, group_hits, group_misses).astype(jnp.bfloat16)
-    return (context.reshape(1, TPW * miss_rows, head_dev * LATENT_WIDTH), delivered)
+        slot_position = own_owner * push_cap + jnp.sum(same_owner.astype(jnp.int32), axis=1)
+        every_page = jnp.concatenate([cached_pages, new_pages], axis=0)
+        outgoing = pick_rows(slot_position, all_live, every_page, slot_total)
+        delivered = lax.all_to_all(outgoing, "pool", split_axis=0, concat_axis=0, tiled=True)
+    return (context[None], delivered)
 
 
 def solution(mesh):

time: 752 us -> 199 us (0.26)
  waiting for transfers between devices: 514 us -> 11 us
  Pallas kernels: 0 us -> 123 us
  local copies, waits for them, and re-layouts: 105 us -> 38.5 us
  other arithmetic: 74.4 us -> 16.1 us
  matrix products: 29.3 us -> 0 us
  starting transfers between devices: 24.5 us -> 7.48 us
    all_to_all x1 -> x0, waiting for transfers between devices: 336 us -> none  [shards(): lax.all_to_all(outgoing, 'pool', split_axis=0, concat_axis=0, tiled=True)]
    ppermute x4 -> x0, waiting for transfers between devices: 138 us -> none  [swapped(): return lax.ppermute(value, axis, pairs)]
    pallas_call x0 -> x2, Pallas kernels: none -> 123 us  [the longest x1 102 us: gather_keys(): pl.pallas_call(gather_body, out_shape=jax.ShapeDtypeStruct((TPW,) + own.s...]
    select_n x6 -> x0, other arithmetic: 38.6 us -> none  [the longest x4 37.1 us: shards(): jnp.where(upper, jnp.concatenate([other, block], axis=0), jnp.concatenate...]
    dot_general x3 -> x0, matrix products: 29.3 us -> none  [the longest x1 14 us: attend_block(): jnp.einsum('lgqu,ltu->lqgt', head_queries, latent_keys, preferred_element...]
    all_to_all x1, waiting for transfers between devices: 40 us -> 11 us  [shards(): lax.all_to_all(outbox, 'pool', split_axis=0, concat_axis=0, tiled=True)]
    ppermute x4 -> x0, local copies, waits for them, and re-layouts: 26 us -> none  [swapped(): return lax.ppermute(value, axis, pairs)]
    select_n x3 -> x0, local copies, waits for them, and re-layouts: 23.7 us -> none  [shards(): jnp.where(upper, jnp.concatenate([other, block], axis=0), jnp.concatenate...]
  transfers between devices with their start and end apart: 6 -> 1, of which waited for: 5 -> 1; matrix products, arithmetic and copies ran while one was open for 5% -> 17% of each run, Pallas kernels for 0% -> 0%
where the time goes in v1:
time: 199 us; the launch traced here: 198 us
  Pallas kernels  123 us (62%)
  local copies, waits for them, and re-layouts  38.5 us (19%)
  other arithmetic  16.1 us (8%)
  waiting for transfers between devices  11 us (6%)
  starting transfers between devices  7.48 us (4%)
    pallas_call x1, Pallas kernels, gather_keys(): pl.pallas_call(gather_body, out_shape=jax.ShapeDtypeStruct((TPW,) + own.s...  102 us
    pallas_call x1, Pallas kernels, attend(): pl.pallas_call(functools.partial(attend_body, key_count, miss_rows), grid...  21.5 us
    reshape x1, local copies, waits for them, and re-layouts, shards(): query_rows = queries.reshape(TPW, -1, head_dev, features)  11.5 us
    all_to_all x1, waiting for transfers between devices, shards(): lax.all_to_all(outbox, 'pool', split_axis=0, concat_axis=0, tiled=True)  11 us
    unnamed x19, local copies, waits for them, and re-layouts  9.27 us
    all_to_all x1, starting transfers between devices, shards(): lax.all_to_all(outbox, 'pool', split_axis=0, concat_axis=0, tiled=True)  7.48 us
    slice x1, local copies, waits for them, and re-layouts, turn_queries(): latent = by_head(query_rows[..., :LATENT_WIDTH])  5.79 us
  transfers between devices with their start and end apart: 1, of which 1 were waited for; matrix products, arithmetic and copies ran while one was open for 17% of the time, Pallas kernels for 0%

profile of v1, /device:TPU:1, one launch (start us, length us, event | category | flops | bytes accessed | tf_op | source)
XLA Modules:
  0.0 198.0 jit_solution(6585832619593464933)
XLA Ops:
  0.6 0.0 copy-start
  0.7 0.9 fusion.23
  1.6 0.2 reduce_window_sum.23
  1.8 0.2 fusion.9
  1.9 0.9 select_reduce_fusion
  2.8 0.1 copy.21
  2.9 0.1 copy.22
  3.0 0.1 reshape.279
  3.1 0.0 copy-done
  3.1 1.7 gather_fusion
  4.8 1.7 gather.9
  6.5 3.4 %broadcast_select_fusion = bf16[16,6,9216]{2,1,0:T(8,128)(2,1)} fusion(bf16[16,6,9216]{2,1,0:T(8,128)(2,1)} %gather.9, pred[16,6]{1,0:T(8,128)(4,1)S(1)} %copy.21), kind=kLoop, calls=%fused_computation.6 | loop fusion | flops 884736 | bytes 3539040 | tf_op jit(solution)/shard_map/jit(_where)/select_n | solution.py:321
  10.0 0.0 copy-start.4
  10.0 7.5 %all-to-all-start = ((bf16[16,6,9216]{2,1,0:T(8,128)(2,1)}), bf16[16,6,9216]{2,1,0:T(8,128)(2,1)}, u32[]{:S(2)}, u32[]{:S(2)}) async-start(bf16[16,6,9216]{2,1,0:T(8,128)(2,1)} %broadcast_select_fusion), calls=%async_computation | async-start | bytes 4718592 | tf_op jit(solution)/shard_map/all_to_all | solution.py:322
  17.5 0.0 copy-done.4
  17.5 0.6 dynamic_slice.12
  18.1 0.7 fusion.21
  18.8 11.5 %reshape.276 = bf16[16,64,4,576]{3,2,1,0:T(4,128)(2,1)} reshape(bf16[1,1024,2304]{2,1,0:T(8,128)(2,1)} %param.9) | data formatting | bytes 9437184 | tf_op jit(solution)/shard_map/reshape | solution.py:352
  30.3 0.0 copy-start.8
  30.3 5.8 %slice.43 = bf16[16,64,4,512]{3,2,1,0:T(4,128)(2,1)} slice(bf16[16,64,4,576]{3,2,1,0:T(4,128)(2,1)} %reshape.276), slice={[0:16], [0:64], [0:4], [0:512]} | slice | bytes 8388608 | tf_op jit(solution)/shard_map/slice | solution.py:69
  36.7 0.0 copy-done.8
  36.7 0.6 dynamic_slice.14
  37.3 0.1 broadcast_compare_fusion.1
  37.4 0.0 copy-done.7
  37.4 0.0 copy-done.6
  37.4 0.1 fusion.24
  37.5 0.2 reduce_window_sum.22
  37.7 0.1 select_reduce_fusion.1
  37.9 0.1 copy.18
  38.0 0.1 sub.27.picks
  38.1 0.0 copy-done.5
  38.1 0.1 reshape.287
  38.2 0.0 slice-start
  38.2 5.5 %copy.26 = bf16[16,64,4,512]{3,1,2,0:T(8,128)(2,1)} copy(bf16[16,64,4,512]{3,2,1,0:T(4,128)(2,1)} %slice.43) | data formatting | bytes 8388608
  43.7 0.6 iota_compare_fusion.8
  44.3 0.6 iota_compare_fusion.7
  44.9 0.2 convert_reduce_fusion
  45.1 1.4 fusion.20
  46.4 0.1 multiply_reduce_fusion
  46.5 0.1 add_convert_fusion.1
  46.6 1.9 multiply_cosine_fusion
  48.5 0.0 slice-done
  48.5 0.3 copy_convert_fusion
  48.8 0.9 subtract_convert_fusion
  49.7 0.6 pad_maximum_fusion
  50.3 0.2 fusion.14
  50.5 0.1 multiply_multiply_fusion
  50.6 0.1 fusion.7
  50.7 1.9 fusion.2.pq
  52.6 11.0 %all-to-all-done = bf16[16,6,9216]{2,1,0:T(8,128)(2,1)} async-done(((bf16[16,6,9216]{2,1,0:T(8,128)(2,1)}), bf16[16,6,9216]{2,1,0:T(8,128)(2,1)}, u32[]{:S(2)}, u32[]{:S(2)}) %all-to-all-start) | async-done | bytes 1769504 | tf_op jit(solution)/shard_map/all_to_all | solution.py:322
  63.6 2.0 all_to_all.7
  65.6 1.1 gather_fusion.1
  66.7 0.8 reshape.280
  67.5 0.1 fusion.3
  67.6 0.1 copy.23
  67.7 0.1 copy.24
  67.9 1.0 pad_maximum_fusion.1.own
  68.9 101.9 %shard_map.104.keys = bf16[16,960,512]{2,1,0:T(8,128)(2,1)} custom-call(bf16[960,512]{1,0:T(8,128)(2,1)} %pad_maximum_fusion.1.own), custom_call_target="tpu_custom_call" | custom-call | tf_op jit(solution)/shard_map/pallas_call | solution.py:191
  170.8 0.0 copy-start.2
  170.8 2.2 %copy-done.2 = bf16[16,64,4,512]{3,1,2,0:T(8,128)(2,1)S(1)} copy-done((bf16[16,64,4,512]{3,1,2,0:T(8,128)(2,1)S(1)}, bf16[16,64,4,512]{3,1,2,0:T(8,128)(2,1)}, u32[]{:S(2)}) %copy-start.2) | copy-done | bytes 4194328
  173.0 1.6 copy-done.3
  174.6 21.5 %shard_map.105 = (bf16[1024,2048]{1,0:T(8,128)(2,1)}, bf16[16,4,16,576]{3,2,1,0:T(8,128)(2,1)S(1)}) custom-call(s32[16]{0:T(128)S(1)} %copy-done.4, s32[16]{0:T(128)S(1)} %get-tuple-element.18.misses, s32[64]{0:T(128)S(1)} %sub.27.picks, bf16[16,256,512]{2,1,0:T(8,128)(2,1)S(1)} %bitcast.34, bf16[16,512,128]{2,1,0:T(8,128)(2,1)S(1)} %copy-done.3, ...), custom_call_target="tpu_custom_call" | custom-call | tf_op jit(solution)/shard_map/pallas_call | solution.py:273
  196.1 2.0 reshape.285
  198.0 0.0 copy-done.1
  (20 shorter events, 0.1 us)
Async XLA Ops:
  0.6 2.5 %copy-start = (bf16[96,9216]{1,0:T(8,128)(2,1)S(1)}, bf16[96,9216]{1,0:T(8,128)(2,1)}, u32[]{:S(2)}) copy-start(bf16[96,9216]{1,0:T(8,128)(2,1)} %param.10) | copy-start | bytes 5308420
  10.0 7.5 %copy-start.4 = (s32[16]{0:T(128)S(1)}, s32[16]{0:T(128)}, u32[]{:S(2)}) copy-start(s32[16]{0:T(128)} %hits) | copy-start | bytes 196
  10.0 53.6 %all-to-all-start = ((bf16[16,6,9216]{2,1,0:T(8,128)(2,1)}), bf16[16,6,9216]{2,1,0:T(8,128)(2,1)}, u32[]{:S(2)}, u32[]{:S(2)}) async-start(bf16[16,6,9216]{2,1,0:T(8,128)(2,1)} %broadcast_select_fusion), calls=%async_computation | async-start | bytes 4718592 | tf_op jit(solution)/shard_map/all_to_all | solution.py:322
  30.3 6.5 %copy-start.8 = (s32[16]{0:T(128)S(1)}, s32[16]{0:T(128)}, u32[]{:S(2)}) copy-start(s32[16]{0:T(128)} %param.14) | copy-start | bytes 196
  30.3 7.1 %copy-start.7 = (bf16[512]{0:T(512)(128)(2,1)S(1)}, bf16[512]{0:T(512)(128)(2,1)}, u32[]{:S(2)}) copy-start(bf16[512]{0:T(512)(128)(2,1)} %param.12) | copy-start | bytes 3076
  30.3 7.1 %copy-start.6 = (s32[16,52,1]{1,2,0:T(1,128)S(1)}, s32[16,52,1]{1,2,0:T(1,128)}, u32[]{:S(2)}) copy-start(s32[16,52,1]{1,2,0:T(1,128)} %param.17) | copy-start | bytes 9988
  30.3 7.8 %copy-start.5 = (bf16[4,9216]{1,0:T(4,128)(2,1)S(1)}, bf16[4,9216]{1,0:T(4,128)(2,1)}, u32[]{:S(2)}) copy-start(bf16[4,9216]{1,0:T(4,128)(2,1)} %param.11) | copy-start | bytes 221188
  38.2 10.3 %slice-start = ((bf16[16,64,4,576]{3,2,1,0:T(4,128)(2,1)}), bf16[16,64,4,64]{3,2,1,0:T(4,128)(2,1)S(1)}, s32[]{:S(2)}) async-start(bf16[16,64,4,576]{3,2,1,0:T(4,128)(2,1)} %reshape.276), calls=%async_computation.1 | async-start | bytes 2097152 | tf_op jit(solution)/shard_map/slice | solution.py:65
  170.8 2.2 %copy-start.2 = (bf16[16,64,4,512]{3,1,2,0:T(8,128)(2,1)S(1)}, bf16[16,64,4,512]{3,1,2,0:T(8,128)(2,1)}, u32[]{:S(2)}) copy-start(bf16[16,64,4,512]{3,1,2,0:T(8,128)(2,1)} %copy.26) | copy-start | bytes 12582916
  173.0 1.6 copy-start.3
  174.6 23.5 %copy-start.1 = (bf16[96,9216]{1,0:T(8,128)(2,1)S(1)}, bf16[96,9216]{1,0:T(8,128)(2,1)}, u32[]{:S(2)}) copy-start(bf16[96,9216]{1,0:T(8,128)(2,1)} %param.10) | copy-start | bytes 5308420

commit v2 on v0

--- a/solution.py
+++ b/solution.py
@@ -1,23 +1,23 @@
+import functools
+
 import jax
 import jax.numpy as jnp
 from jax import lax
+from jax.experimental import pallas as pl
+from jax.experimental.pallas import tpu as pltpu
 from jax.sharding import PartitionSpec as P
 
 LATENT_WIDTH = 512
 ROPE = 64
 PAGE = 16
 TPW = 16
+PACK = 128
+MESH = pl.DeviceIdType.MESH
 
 
 score_scale = 0.07216878364870323
 rope_base = 10000.0
 norm_eps = 1e-06
-
-
-def swapped(value, axis, stride):
-    mask = 2**stride
-    pairs = [(source, source ^ mask) for source in range(lax.axis_size(axis))]
-    return lax.ppermute(value, axis, pairs)
 
 
 def rope_tables(positions, rotary_width):
@@ -65,38 +65,232 @@
     turned = rotate(query_rows[..., LATENT_WIDTH:].astype(jnp.float32), cosine, sine_table).astype(
         jnp.bfloat16
     )
-    return jnp.concatenate([query_rows[..., :LATENT_WIDTH], turned], axis=3)
-
-
-def attend_block(head_queries, latent_keys, hits, misses):
-    row_count = head_queries.shape[1]
-    key_count = latent_keys.shape[1]
-    cached_rows = key_count - row_count
-    row_steps = jnp.arange(row_count)
-    key_steps = jnp.arange(key_count)
-    cached_live = key_steps[None, :] // PAGE < hits[:, None]
-    fresh_steps = key_steps - cached_rows
-    fresh_live = (fresh_steps[None, None, :] <= row_steps[None, :, None]) & (
-        fresh_steps[None, None, :] < misses[:, None, None]
-    )
-    allowed = jnp.where(
-        (key_steps < cached_rows)[None, None, :], cached_live[:, None, :], fresh_live
-    )
-    scores = (
-        jnp.einsum("lgqu,ltu->lqgt", head_queries, latent_keys, preferred_element_type=jnp.float32)
-        * score_scale
-    )
-    scores = jnp.where(allowed[:, None, :, :], scores, -jnp.inf)
-    row_max = jnp.max(scores, axis=3, keepdims=True)
+    by_head = lambda value: value.transpose(0, 2, 1, 3).reshape(batch, -1, value.shape[-1])
+    latent = by_head(query_rows[..., :LATENT_WIDTH])
+    rotary = by_head(turned)
+    blank = jnp.zeros_like(rotary)
+    paired = jnp.concatenate(
+        [jnp.concatenate([rotary, blank], axis=2), jnp.concatenate([blank, rotary], axis=2)], axis=1
+    )
+    return latent, paired
+
+
+def pack_keys(keys):
+    rotary = keys[:, LATENT_WIDTH:]
+    spare = PACK * (LATENT_WIDTH // ROPE) - keys.shape[0]
+    rotary = jnp.concatenate([rotary, jnp.zeros((spare, ROPE), keys.dtype)], axis=0)
+    packed = rotary.reshape(-1, PACK, ROPE).transpose(1, 0, 2).reshape(PACK, LATENT_WIDTH)
+    return jnp.concatenate([keys[:, :LATENT_WIDTH], packed], axis=0)
+
+
+def attend_one(latent_queries, paired_queries, keys, hits, misses, key_count, miss_rows):
+    rows = latent_queries.shape[0]
+    cached_rows = key_count - miss_rows
+    contract = (((1,), (1,)), ((), ()))
+    latent_keys = keys[:key_count, :]
+    scores = lax.dot_general(
+        latent_queries, latent_keys, contract, preferred_element_type=jnp.float32
+    )
+    parts = []
+    for pair in range(LATENT_WIDTH // 128):
+        if pair * 2 * PACK >= key_count:
+            break
+        both = lax.dot_general(
+            paired_queries,
+            keys[key_count:, pair * 128 : (pair + 1) * 128],
+            contract,
+            preferred_element_type=jnp.float32,
+        )
+        parts += [both[:rows], both[rows:]]
+    rotary = jnp.concatenate(parts, axis=1)[:, :key_count]
+    scores = (scores + rotary) * score_scale
+    row_steps = lax.rem(lax.broadcasted_iota(jnp.int32, (rows, 1), 0), miss_rows)
+    key_steps = lax.broadcasted_iota(jnp.int32, (rows, key_count), 1)
+    fresh_end = cached_rows + jnp.minimum(row_steps + 1, misses)
+    allowed = (key_steps < hits * PAGE) | ((key_steps >= cached_rows) & (key_steps < fresh_end))
+    scores = jnp.where(allowed, scores, -jnp.inf)
+    row_max = jnp.max(scores, axis=1, keepdims=True)
     weights = jnp.exp(scores - row_max)
-    attention_weights = (weights / jnp.sum(weights, axis=3, keepdims=True)).astype(jnp.bfloat16)
-    context = jnp.einsum(
-        "rylp,rpj->rlyj",
-        attention_weights,
-        latent_keys[:, :, :LATENT_WIDTH],
-        preferred_element_type=jnp.float32,
-    )
-    return jnp.where((row_steps[None, :] < misses[:, None])[:, :, None, None], context, 0.0)
+    total = jnp.sum(weights, axis=1, keepdims=True)
+    context = jnp.dot(
+        weights.astype(jnp.bfloat16), latent_keys, preferred_element_type=jnp.float32
+    )
+    return jnp.where(row_steps < misses, context / total, 0.0)
+
+
+def serve_body(
+    key_count, miss_rows, hits, misses, own, lq, pq, rows_sel, context, pages, keys, *sems
+):
+    local_sem, up_sem, down_sem, y_sem, core_sem, recv_sem = sems
+    me = lax.axis_index("pool")
+    member = lax.rem(me, TPW)
+    base = me - member
+    z, y, c = member // 4, lax.rem(member // 2, 2), lax.rem(member, 2)
+
+    def slot_of(zz, yy, cc):
+        return zz * 4 + yy * 2 + cc
+
+    across = base + slot_of(z, 1 - y, c)
+    twin = base + slot_of(z, y, 1 - c)
+    above = base + slot_of(lax.rem(z + 1, 4), y, c)
+    below = base + slot_of(lax.rem(z + 3, 4), y, c)
+    has_up, has_down = z < 3, z > 0
+
+    barrier = pltpu.get_barrier_semaphore()
+    pl.semaphore_signal(barrier, inc=1, device_id={"pool": across}, device_id_type=MESH)
+    pl.semaphore_signal(barrier, inc=1, device_id={"pool": twin}, device_id_type=MESH)
+
+    @pl.when(has_up)
+    def _():
+        pl.semaphore_signal(barrier, inc=1, device_id={"pool": above}, device_id_type=MESH)
+
+    @pl.when(has_down)
+    def _():
+        pl.semaphore_signal(barrier, inc=1, device_id={"pool": below}, device_id_type=MESH)
+
+    mine = pltpu.make_async_copy(own, keys.at[member], local_sem)
+    mine.start()
+    pl.semaphore_wait(barrier, 2 + has_up.astype(jnp.int32) + has_down.astype(jnp.int32))
+    mine.wait()
+
+    def copy(zz, yy, cc, sem, device):
+        slot = slot_of(zz, yy, cc)
+        return pltpu.make_async_remote_copy(
+            src_ref=keys.at[slot],
+            dst_ref=keys.at[slot],
+            send_sem=sem,
+            recv_sem=recv_sem.at[slot],
+            device_id={"pool": device},
+            device_id_type=MESH,
+        )
+
+    def arrive(zz, yy, cc):
+        copy(zz, yy, cc, core_sem.at[0], twin).wait_recv()
+
+    def column(zz, act):
+        @pl.when((zz <= z) & has_up)
+        def _():
+            act(copy(zz, y, c, up_sem.at[zz], above))
+
+        @pl.when((zz >= z) & has_down)
+        def _():
+            act(copy(zz, y, c, down_sem.at[zz], below))
+
+        act(copy(zz, y, c, y_sem.at[zz], across))
+        act(copy(zz, y, c, core_sem.at[zz * 2 + y], twin))
+
+    def work(slot):
+        block = keys.at[slot]
+        result = attend_one(
+            lq[slot], pq[slot], block, hits[slot], misses[slot], key_count, miss_rows
+        ).astype(context.dtype)
+        place = pl.ds(pl.multiple_of(slot * miss_rows, miss_rows), miss_rows)
+        for head in range(result.shape[0] // miss_rows):
+            context[place, head * LATENT_WIDTH : (head + 1) * LATENT_WIDTH] = result[
+                head * miss_rows : (head + 1) * miss_rows
+            ]
+        wide = -(-key_count // PACK) * PACK
+        chosen = rows_sel[slot] == lax.broadcasted_iota(
+            jnp.int32, (rows_sel.shape[1], wide), 1
+        )
+        chosen = chosen.astype(jnp.bfloat16)
+        latent = jnp.dot(
+            chosen[:, :key_count], block[:key_count, :], preferred_element_type=jnp.float32
+        )
+        sums = [jnp.zeros((rows_sel.shape[1], 128), jnp.float32)] * 2
+        for chunk in range(wide // PACK):
+            pair = chunk // 2
+            sums[chunk % 2] += jnp.dot(
+                chosen[:, chunk * PACK : (chunk + 1) * PACK],
+                block[key_count:, pair * 128 : (pair + 1) * 128],
+                preferred_element_type=jnp.float32,
+            )
+        rotary = sums[0][:, :ROPE] + sums[1][:, ROPE:]
+        pages[slot, :, :LATENT_WIDTH] = latent.astype(pages.dtype)
+        pages[slot, :, LATENT_WIDTH:] = rotary.astype(pages.dtype)
+
+    def place_of(distance, way):
+        zz = z + jnp.where(way == 0, -distance, distance)
+        inside = (zz >= 0) & (zz <= 3) & (distance >= 0) & (distance <= 3)
+        return jnp.clip(zz, 0, 3), inside & ((distance > 0) | (way == 0))
+
+    def step(distance, carry):
+        for way in range(2):
+            zz, inside = place_of(distance, way)
+
+            @pl.when(inside)
+            def _():
+                @pl.when(distance > 0)
+                def _():
+                    arrive(zz, y, c)
+
+                column(zz, lambda item: item.start())
+
+        for way in range(2):
+            zz, inside = place_of(distance - 1, way)
+
+            @pl.when(inside)
+            def _():
+                arrive(zz, 1 - y, c)
+                copy(zz, 1 - y, c, core_sem.at[zz * 2 + 1 - y], twin).start()
+
+        def one(index, carry):
+            way = lax.rem(index, 2)
+            cc = lax.rem(c + lax.rem(index // 2, 2), 2)
+            side = index // 4
+            yy = lax.rem(y + side, 2)
+            zz, inside = place_of(distance - side, way)
+
+            @pl.when(inside)
+            def _():
+                @pl.when(cc != c)
+                def _():
+                    arrive(zz, yy, cc)
+
+                work(slot_of(zz, yy, cc))
+
+            return carry
+
+        return lax.fori_loop(0, 8, one, carry)
+
+    lax.fori_loop(0, 5, step, 0)
+
+    def finish(zz, carry):
+        column(zz, lambda item: item.wait_send())
+        copy(zz, 1 - y, c, core_sem.at[zz * 2 + 1 - y], twin).wait_send()
+        return carry
+
+    lax.fori_loop(0, 4, finish, 0)
+
+
+def serve(own, latent_queries, paired_queries, hits, misses, picks, key_count, miss_rows):
+    prompts, rows, _ = latent_queries.shape
+    heads = rows // miss_rows
+    picked = picks[:, :, None] * PAGE + jnp.arange(PAGE)
+    picked = jnp.where(picks[:, :, None] >= 0, picked, -1).reshape(prompts, -1, 1)
+    vmem = pl.BlockSpec(memory_space=pltpu.VMEM)
+    smem = pl.BlockSpec(memory_space=pltpu.SMEM)
+    return pl.pallas_call(
+        functools.partial(serve_body, key_count, miss_rows),
+        out_shape=[
+            jax.ShapeDtypeStruct((prompts * miss_rows, heads * LATENT_WIDTH), jnp.bfloat16),
+            jax.ShapeDtypeStruct((prompts, picked.shape[1], LATENT_WIDTH + ROPE), jnp.bfloat16),
+        ],
+        in_specs=[smem, smem, vmem, vmem, vmem, vmem],
+        out_specs=[vmem, vmem],
+        scratch_shapes=[
+            pltpu.VMEM((TPW,) + own.shape, own.dtype),
+            pltpu.SemaphoreType.DMA,
+            pltpu.SemaphoreType.DMA((4,)),
+            pltpu.SemaphoreType.DMA((4,)),
+            pltpu.SemaphoreType.DMA((4,)),
+            pltpu.SemaphoreType.DMA((8,)),
+            pltpu.SemaphoreType.DMA((TPW,)),
+        ],
+        compiler_params=pltpu.CompilerParams(
+            collective_id=0, has_side_effects=True, vmem_limit_bytes=48 * 1024 * 1024
+        ),
+    )(hits, misses, own, latent_queries, paired_queries, picked)
 
 
 def shards(
@@ -149,18 +343,6 @@
     push_cap = max(2, (total + pool_size - 1) // pool_size)
     slot_total = pool_size * push_cap
     new_steps = jnp.arange(per_prompt)
-    fresh_live = new_steps * PAGE < own_miss
-    all_live = jnp.concatenate([own_live, fresh_live], axis=0)
-    all_steps = jnp.arange(total)
-    same_owner = (
-        (all_steps[None, :] < all_steps[:, None])
-        & (own_owner[None, :] == own_owner[:, None])
-        & all_live[None, :]
-    )
-    slot_position = own_owner * push_cap + jnp.sum(same_owner.astype(jnp.int32), axis=1)
-    every_page = jnp.concatenate([cached_pages, new_pages], axis=0)
-    outgoing = pick_rows(slot_position, all_live, every_page, slot_total)
-    delivered = lax.all_to_all(outgoing, "pool", split_axis=0, concat_axis=0, tiled=True)
     own_keys = jnp.concatenate([cached_pages.reshape(pages_max * PAGE, features), new_keys], axis=0)
     member = device_index % TPW
     group_base = device_index - member
@@ -169,16 +351,40 @@
     head_dev = queries.shape[2] // features
     query_rows = queries.reshape(TPW, -1, head_dev, features)
     miss_rows = query_rows.shape[1]
-    head_queries = turn_queries(query_rows, group_hits)
-    block = own_keys[None]
-    for bit in range(TPW.bit_length() - 1):
-        other = swapped(block, "pool", bit)
-        upper = member // (1 << bit) % 2 == 1
-        block = jnp.where(
-            upper, jnp.concatenate([other, block], axis=0), jnp.concatenate([block, other], axis=0)
+    latent_queries, paired_queries = turn_queries(query_rows, group_hits)
+    group_owner = lax.dynamic_slice_in_dim(page_owner[:, :, 0], group_base, TPW)
+    group_live = jnp.concatenate(
+        [page_steps < group_hits[:, None], new_steps * PAGE < group_misses[:, None]], axis=1
+    )
+    taken = group_live & (group_owner == device_index)
+    rank = jnp.cumsum(taken.astype(jnp.int32), axis=1) - 1
+    all_steps = jnp.arange(total)
+    hit = taken[:, None, :] & (rank[:, None, :] == jnp.arange(push_cap)[None, :, None])
+    picks = jnp.sum(jnp.where(hit, all_steps + 1, 0), axis=2) - 1
+    context, pages = serve(
+        pack_keys(own_keys),
+        latent_queries,
+        paired_queries,
+        group_hits,
+        group_misses,
+        picks,
+        own_keys.shape[0],
+        miss_rows,
+    )
+    if pool_size == TPW:
+        delivered = pages.reshape(slot_total, PAGE * features)
+    else:
+        all_live = jnp.concatenate([own_live, new_steps * PAGE < own_miss], axis=0)
+        same_owner = (
+            (all_steps[None, :] < all_steps[:, None])
+            & (own_owner[None, :] == own_owner[:, None])
+            & all_live[None, :]
         )
-    context = attend_block(head_queries, block, group_hits, group_misses).astype(jnp.bfloat16)
-    return (context.reshape(1, TPW * miss_rows, head_dev * LATENT_WIDTH), delivered)
+        slot_position = own_owner * push_cap + jnp.sum(same_owner.astype(jnp.int32), axis=1)
+        every_page = jnp.concatenate([cached_pages, new_pages], axis=0)
+        outgoing = pick_rows(slot_position, all_live, every_page, slot_total)
+        delivered = lax.all_to_all(outgoing, "pool", split_axis=0, concat_axis=0, tiled=True)
+    return (context[None], delivered)
 
 
 def solution(mesh):

time: 752 us -> 195 us (0.26)
  waiting for transfers between devices: 514 us -> 9.15 us
  Pallas kernels: 0 us -> 106 us
  local copies, waits for them, and re-layouts: 105 us -> 49.8 us
  other arithmetic: 74.4 us -> 19.7 us
  matrix products: 29.3 us -> 0 us
  starting transfers between devices: 24.5 us -> 7.48 us
    all_to_all x1 -> x0, waiting for transfers between devices: 336 us -> none  [shards(): lax.all_to_all(outgoing, 'pool', split_axis=0, concat_axis=0, tiled=True)]
    ppermute x4 -> x0, waiting for transfers between devices: 138 us -> none  [swapped(): return lax.ppermute(value, axis, pairs)]
    pallas_call x0 -> x1, Pallas kernels: none -> 106 us  [serve(): pl.pallas_call(functools.partial(serve_body, key_count, miss_rows), out_s...]
    select_n x6 -> x1, other arithmetic: 38.6 us -> 0.15 us  [serve(): jnp.where(picks[:, :, None] >= 0, picked, -1).reshape(prompts, -1, 1)]
    all_to_all x1, waiting for transfers between devices: 40 us -> 9.15 us  [shards(): lax.all_to_all(outbox, 'pool', split_axis=0, concat_axis=0, tiled=True)]
    dot_general x3 -> x0, matrix products: 29.3 us -> none  [the longest x1 14 us: attend_block(): jnp.einsum('lgqu,ltu->lqgt', head_queries, latent_keys, preferred_element...]
    ppermute x4 -> x0, local copies, waits for them, and re-layouts: 26 us -> none  [swapped(): return lax.ppermute(value, axis, pairs)]
    select_n x3 -> x0, local copies, waits for them, and re-layouts: 23.7 us -> none  [shards(): jnp.where(upper, jnp.concatenate([other, block], axis=0), jnp.concatenate...]
  transfers between devices with their start and end apart: 6 -> 1, of which waited for: 5 -> 1; matrix products, arithmetic and copies ran while one was open for 5% -> 19% of each run, Pallas kernels for 0% -> 0%
where the time goes in v2:
time: 195 us; the launch traced here: 194 us
  Pallas kernels  106 us (54%)
  local copies, waits for them, and re-layouts  49.8 us (26%)
  other arithmetic  19.7 us (10%)
  waiting for transfers between devices  9.15 us (5%)
  starting transfers between devices  7.48 us (4%)
    pallas_call x1, Pallas kernels, serve(): pl.pallas_call(functools.partial(serve_body, key_count, miss_rows), out_s...  106 us
    unnamed x18, local copies, waits for them, and re-layouts  13 us
    reshape x1, local copies, waits for them, and re-layouts, shards(): query_rows = queries.reshape(TPW, -1, head_dev, features)  11.5 us
    all_to_all x1, waiting for transfers between devices, shards(): lax.all_to_all(outbox, 'pool', split_axis=0, concat_axis=0, tiled=True)  9.15 us
    all_to_all x1, starting transfers between devices, shards(): lax.all_to_all(outbox, 'pool', split_axis=0, concat_axis=0, tiled=True)  7.48 us
    slice x1, local copies, waits for them, and re-layouts, turn_queries(): latent = by_head(query_rows[..., :LATENT_WIDTH])  5.77 us
    gather x1, local copies, waits for them, and re-layouts, shards(): cached_pages = arrived[source]  4.51 us
  transfers between devices with their start and end apart: 1, of which 1 were waited for; matrix products, arithmetic and copies ran while one was open for 19% of the time, Pallas kernels for 0%

profile of v2, /device:TPU:1, one launch (start us, length us, event | category | flops | bytes accessed | tf_op | source)
XLA Modules:
  0.0 194.0 jit_solution(5196083176719106499)
XLA Ops:
  0.6 0.0 copy-start
  0.6 0.9 fusion.24
  1.6 0.2 reduce_window_sum.22
  1.8 0.2 fusion.9
  1.9 0.9 select_reduce_fusion
  2.8 0.1 copy.20
  2.9 0.1 copy.21
  3.0 0.1 reshape.328
  3.1 0.0 copy-done
  3.1 1.7 gather_fusion
  4.8 1.7 gather.9
  6.5 3.5 %broadcast_select_fusion = bf16[16,6,9216]{2,1,0:T(8,128)(2,1)} fusion(bf16[16,6,9216]{2,1,0:T(8,128)(2,1)} %gather.9, pred[16,6]{1,0:T(8,128)(4,1)S(1)} %copy.20), kind=kLoop, calls=%fused_computation.6 | loop fusion | flops 884736 | bytes 3539040 | tf_op jit(solution)/shard_map/jit(_where)/select_n | solution.py:321
  10.0 7.5 %all-to-all-start = ((bf16[16,6,9216]{2,1,0:T(8,128)(2,1)}), bf16[16,6,9216]{2,1,0:T(8,128)(2,1)}, u32[]{:S(2)}, u32[]{:S(2)}) async-start(bf16[16,6,9216]{2,1,0:T(8,128)(2,1)} %broadcast_select_fusion), calls=%async_computation | async-start | bytes 4718592 | tf_op jit(solution)/shard_map/all_to_all | solution.py:322
  17.5 0.0 copy-done.3
  17.5 0.6 dynamic_slice.12
  18.1 0.7 fusion.21
  19.4 0.7 iota_compare_fusion.8
  20.1 0.6 dynamic_slice.14
  20.8 0.1 broadcast_compare_fusion.1
  20.9 0.1 fusion.23
  20.9 0.2 reduce_window_sum.23
  21.1 0.1 select_reduce_fusion.1
  21.3 11.5 %reshape.334 = bf16[16,64,4,576]{3,2,1,0:T(4,128)(2,1)} reshape(bf16[1,1024,2304]{2,1,0:T(8,128)(2,1)} %param.9) | data formatting | bytes 9437184 | tf_op jit(solution)/shard_map/reshape | solution.py:352
  32.8 5.8 %slice.48 = bf16[16,64,4,512]{3,2,1,0:T(4,128)(2,1)} slice(bf16[16,64,4,576]{3,2,1,0:T(4,128)(2,1)} %reshape.334), slice={[0:16], [0:64], [0:4], [0:512]} | slice | bytes 8388608 | tf_op jit(solution)/shard_map/slice | solution.py:69
  38.6 0.1 add.167
  38.7 0.1 copy.26
  38.8 0.1 copy.27
  38.9 0.1 broadcast_in_dim.106
  39.0 0.3 broadcast_in_dim.110
  39.3 0.1 reshape.339
  39.5 0.1 add.164
  39.5 0.3 add.170
  39.9 0.0 slice-start
  39.9 5.5 %copy.31 = bf16[16,64,4,512]{3,1,2,0:T(8,128)(2,1)} copy(bf16[16,64,4,512]{3,2,1,0:T(4,128)(2,1)} %slice.48) | data formatting | bytes 8388608
  45.4 0.6 iota_compare_fusion.7
  46.0 0.2 convert_reduce_fusion
  46.2 1.4 fusion.20
  47.5 0.1 multiply_reduce_fusion
  47.7 0.1 add_convert_fusion.1
  47.7 1.9 multiply_cosine_fusion
  49.6 0.3 copy_convert_fusion
  49.9 0.9 subtract_convert_fusion
  50.8 0.6 pad_maximum_fusion
  51.4 0.2 fusion.14
  51.6 0.1 multiply_multiply_fusion
  51.7 0.7 fusion.7
  52.4 1.9 fusion.2.pq
  54.3 0.1 add_select_fusion.rows_sel
  54.5 9.1 %all-to-all-done = bf16[16,6,9216]{2,1,0:T(8,128)(2,1)} async-done(((bf16[16,6,9216]{2,1,0:T(8,128)(2,1)}), bf16[16,6,9216]{2,1,0:T(8,128)(2,1)}, u32[]{:S(2)}, u32[]{:S(2)}) %all-to-all-start) | async-done | bytes 1769504 | tf_op jit(solution)/shard_map/all_to_all | solution.py:322
  63.6 2.9 %all_to_all.7 = bf16[96,9216]{1,0:T(8,128)(2,1)} reshape(bf16[16,6,9216]{2,1,0:T(8,128)(2,1)} %all-to-all-done) | data formatting | bytes 3538944 | tf_op jit(solution)/shard_map/all_to_all | solution.py:322
  66.5 4.5 %gather_fusion.1 = bf16[48,9216]{1,0:T(8,128)(2,1)} fusion(bf16[96,9216]{1,0:T(8,128)(2,1)} %all_to_all.7, s32[1024]{0:T(1024)S(1)} %pad_clamp_fusion), kind=kCustom, calls=%fused_computation.1 | custom fusion | bytes 1769664 | tf_op jit(solution)/shard_map/gather | solution.py:335
  71.0 2.0 %reshape.329 = bf16[768,576]{1,0:T(8,128)(2,1)S(1)} reshape(bf16[48,9216]{1,0:T(8,128)(2,1)} %gather_fusion.1) | data formatting | bytes 1769472 | tf_op jit(solution)/shard_map/reshape | solution.py:346
  73.0 0.8 fusion.6
  73.8 1.8 fusion.3
  75.6 0.1 copy.22
  75.8 0.1 copy.23
  75.9 1.2 pad_maximum_fusion.1.own
  77.1 0.0 copy-start.1
  77.1 1.6 copy-done.1
  78.7 106.3 %shard_map.104 = (bf16[1024,2048]{1,0:T(8,128)(2,1)}, bf16[16,64,576]{2,1,0:T(8,128)(2,1)S(1)}) custom-call(s32[16]{0:T(128)S(1)} %copy-done.3, s32[16]{0:T(128)S(1)} %get-tuple-element.18.misses, bf16[960,512]{1,0:T(8,128)(2,1)S(1)} %pad_maximum_fusion.1.own, bf16[16,256,512]{2,1,0:T(8,128)(2,1)} %bitcast.32, bf16[16,512,128]{2,1,0:T(8,128)(2,1)S(1)} %copy-done.1, ...), custom_call_target="tpu_custom_call" | custom-call | tf_op jit(solution)/shard_map/pallas_call | solution.py:273
  185.0 0.0 copy-start.2
  185.0 1.0 copy-done.2
  186.1 3.1 %reshape.337 = bf16[64,9216]{1,0:T(8,128)(2,1)} reshape(bf16[16,64,576]{2,1,0:T(8,128)(2,1)} %copy-done.2) | data formatting | bytes 2359296 | tf_op jit(solution)/shard_map/reshape | solution.py:375
  189.2 4.8 %copy.37 = bf16[1,1024,2048]{2,1,0:T(8,128)(2,1)} copy(bf16[1,1024,2048]{2,1,0:T(8,128)(2,1)} %bitcast.34) | data formatting | bytes 8388608
  (26 shorter events, 0.1 us)
Async XLA Ops:
  0.6 2.5 %copy-start = (bf16[96,9216]{1,0:T(8,128)(2,1)S(1)}, bf16[96,9216]{1,0:T(8,128)(2,1)}, u32[]{:S(2)}) copy-start(bf16[96,9216]{1,0:T(8,128)(2,1)} %param.10) | copy-start | bytes 5308420
  10.0 7.5 %copy-start.3 = (s32[16]{0:T(128)S(1)}, s32[16]{0:T(128)}, u32[]{:S(2)}) copy-start(s32[16]{0:T(128)} %hits) | copy-start | bytes 196
  10.0 10.1 %copy-start.7 = (s32[16]{0:T(128)S(1)}, s32[16]{0:T(128)}, u32[]{:S(2)}) copy-start(s32[16]{0:T(128)} %param.14) | copy-start | bytes 196
  10.0 10.8 %copy-start.5 = (s32[16,52,1]{1,2,0:T(1,128)S(1)}, s32[16,52,1]{1,2,0:T(1,128)}, u32[]{:S(2)}) copy-start(s32[16,52,1]{1,2,0:T(1,128)} %param.17) | copy-start | bytes 9988
  10.0 53.6 %all-to-all-start = ((bf16[16,6,9216]{2,1,0:T(8,128)(2,1)}), bf16[16,6,9216]{2,1,0:T(8,128)(2,1)}, u32[]{:S(2)}, u32[]{:S(2)}) async-start(bf16[16,6,9216]{2,1,0:T(8,128)(2,1)} %broadcast_select_fusion), calls=%async_computation | async-start | bytes 4718592 | tf_op jit(solution)/shard_map/all_to_all | solution.py:322
  32.8 5.8 %copy-start.6 = (bf16[512]{0:T(512)(128)(2,1)S(1)}, bf16[512]{0:T(512)(128)(2,1)}, u32[]{:S(2)}) copy-start(bf16[512]{0:T(512)(128)(2,1)} %param.12) | copy-start | bytes 3076
  32.8 6.5 %copy-start.4 = (bf16[4,9216]{1,0:T(4,128)(2,1)S(1)}, bf16[4,9216]{1,0:T(4,128)(2,1)}, u32[]{:S(2)}) copy-start(bf16[4,9216]{1,0:T(4,128)(2,1)} %param.11) | copy-start | bytes 221188
  39.9 9.8 %slice-start = ((bf16[16,64,4,576]{3,2,1,0:T(4,128)(2,1)}), bf16[16,64,4,64]{3,2,1,0:T(4,128)(2,1)S(1)}, s32[]{:S(2)}) async-start(bf16[16,64,4,576]{3,2,1,0:T(4,128)(2,1)} %reshape.334), calls=%async_computation.1 | async-start | bytes 2097152 | tf_op jit(solution)/shard_map/slice | solution.py:65
  77.1 1.6 copy-start.1
  185.0 1.1 copy-start.2

commit v3 on v2

--- a/solution.py
+++ b/solution.py
@@ -121,7 +121,7 @@
 def serve_body(
     key_count, miss_rows, hits, misses, own, lq, pq, rows_sel, context, pages, keys, *sems
 ):
-    local_sem, up_sem, down_sem, y_sem, core_sem, recv_sem = sems
+    local_sem, up_sem, down_sem, y_sem, core_sem, extra_sem, half_sem, recv_sem = sems
     me = lax.axis_index("pool")
     member = lax.rem(me, TPW)
     base = me - member
@@ -135,6 +135,12 @@
     above = base + slot_of(lax.rem(z + 1, 4), y, c)
     below = base + slot_of(lax.rem(z + 3, 4), y, c)
     has_up, has_down = z < 3, z > 0
+    edge_z = jnp.where(z < 2, 0, 3)
+    far_z = 3 - edge_z
+    edge = z == edge_z
+    middle = z != edge_z
+    mate = base + slot_of(z + 1 - 2 * lax.rem(z, 2), y, c)
+    half_rows = own.shape[0] // 2
 
     barrier = pltpu.get_barrier_semaphore()
     pl.semaphore_signal(barrier, inc=1, device_id={"pool": across}, device_id_type=MESH)
@@ -164,6 +170,17 @@
             device_id_type=MESH,
         )
 
+    def half_copy(zz, part, sem, arrived_sem, device, yy):
+        piece = keys.at[slot_of(zz, yy, c), pl.ds(part * half_rows, half_rows)]
+        return pltpu.make_async_remote_copy(
+            src_ref=piece,
+            dst_ref=piece,
+            send_sem=sem,
+            recv_sem=arrived_sem,
+            device_id={"pool": device},
+            device_id_type=MESH,
+        )
+
     def arrive(zz, yy, cc):
         copy(zz, yy, cc, core_sem.at[0], twin).wait_recv()
 
@@ -176,8 +193,36 @@
         def _():
             act(copy(zz, y, c, down_sem.at[zz], below))
 
-        act(copy(zz, y, c, y_sem.at[zz], across))
+        @pl.when((edge & (zz != far_z)) | (middle & (zz != edge_z)))
+        def _():
+            act(copy(zz, y, c, y_sem.at[zz], across))
+
+        @pl.when(edge & (zz == far_z))
+        def _():
+            slot = slot_of(zz, y, c)
+            act(half_copy(zz, 0, y_sem.at[zz], recv_sem.at[slot], across, y))
+
         act(copy(zz, y, c, core_sem.at[zz * 2 + y], twin))
+
+    def extra(zz, act):
+        @pl.when(edge & (zz == edge_z))
+        def _():
+            act(copy(zz, 1 - y, c, extra_sem, mate))
+
+        @pl.when(middle & (zz == far_z))
+        def _():
+            act(half_copy(zz, 1, extra_sem, half_sem, mate, 1 - y))
+
+    def arrive_side(zz):
+        @pl.when((zz != far_z) | middle)
+        def _():
+            arrive(zz, 1 - y, c)
+
+        @pl.when(edge & (zz == far_z))
+        def _():
+            slot = slot_of(zz, 1 - y, c)
+            half_copy(zz, 0, extra_sem, recv_sem.at[slot], mate, 1 - y).wait_recv()
+            half_copy(zz, 1, extra_sem, half_sem, mate, 1 - y).wait_recv()
 
     def work(slot):
         block = keys.at[slot]
@@ -231,7 +276,8 @@
 
             @pl.when(inside)
             def _():
-                arrive(zz, 1 - y, c)
+                arrive_side(zz)
+                extra(zz, lambda item: item.start())
                 copy(zz, 1 - y, c, core_sem.at[zz * 2 + 1 - y], twin).start()
 
         def one(index, carry):
@@ -257,6 +303,7 @@
 
     def finish(zz, carry):
         column(zz, lambda item: item.wait_send())
+        extra(zz, lambda item: item.wait_send())
         copy(zz, 1 - y, c, core_sem.at[zz * 2 + 1 - y], twin).wait_send()
         return carry
 
@@ -285,10 +332,12 @@
             pltpu.SemaphoreType.DMA((4,)),
             pltpu.SemaphoreType.DMA((4,)),
             pltpu.SemaphoreType.DMA((8,)),
+            pltpu.SemaphoreType.DMA,
+            pltpu.SemaphoreType.DMA,
             pltpu.SemaphoreType.DMA((TPW,)),
         ],
         compiler_params=pltpu.CompilerParams(
-            collective_id=0, has_side_effects=True, vmem_limit_bytes=48 * 1024 * 1024
+            collective_id=0, has_side_effects=True, vmem_limit_bytes=36 * 1024 * 1024
         ),
     )(hits, misses, own, latent_queries, paired_queries, picked)
 
@@ -317,8 +366,7 @@
     cap_steps = jnp.arange(slot_cap)
     chosen = held_here[:, None, :] & (held_rank[:, None, :] == cap_steps[None, :, None])
     slot_index = jnp.sum(jnp.where(chosen, page_slot[:, None, :], 0), axis=2).reshape(-1)
-    filled = jnp.any(chosen, axis=2).reshape(-1, 1)
-    outbox = jnp.where(filled, pool_cache[slot_index], jnp.zeros((), pool_cache.dtype))
+    outbox = pool_cache[slot_index]
     arrived = lax.all_to_all(outbox, "pool", split_axis=0, concat_axis=0, tiled=True)
     own_hit = hit_pages[device_index]
     own_miss = misses[device_index]

time: 195 us -> 181 us (0.928)
  Pallas kernels: 106 us -> 92.3 us
  local copies, waits for them, and re-layouts: 49.8 us -> 53.9 us
  other arithmetic: 19.7 us -> 16 us
    pallas_call x1, Pallas kernels: 106 us -> 92.3 us  [serve(): pl.pallas_call(functools.partial(serve_body, key_count, miss_rows), out_s...]
    unnamed x18 -> x22, local copies, waits for them, and re-layouts: 13 us -> 17.1 us
    select_n x2 -> x1, other arithmetic: 3.46 us -> 0.01 us  [shards(): outbox = pool_cache[slot_index]]
    all_to_all x1 -> x2, local copies, waits for them, and re-layouts: 2.9 us -> 4.77 us  [shards(): lax.all_to_all(outbox, 'pool', split_axis=0, concat_axis=0, tiled=True)]
  transfers between devices with their start and end apart: 1 -> 1, of which waited for: 1 -> 1; matrix products, arithmetic and copies ran while one was open for 19% -> 20% of each run, Pallas kernels for 0% -> 0%
where the time goes in v3:
time: 181 us; the launch traced here: 180 us
  Pallas kernels  92.3 us (51%)
  local copies, waits for them, and re-layouts  53.9 us (30%)
  other arithmetic  16 us (9%)
  waiting for transfers between devices  9.16 us (5%)
  starting transfers between devices  7.48 us (4%)
    pallas_call x1, Pallas kernels, serve(): pl.pallas_call(functools.partial(serve_body, key_count, miss_rows), out_s...  92.3 us
    unnamed x22, local copies, waits for them, and re-layouts  17.1 us
    reshape x1, local copies, waits for them, and re-layouts, shards(): query_rows = queries.reshape(TPW, -1, head_dev, features)  11.5 us
    all_to_all x1, waiting for transfers between devices, shards(): lax.all_to_all(outbox, 'pool', split_axis=0, concat_axis=0, tiled=True)  9.16 us
    all_to_all x1, starting transfers between devices, shards(): lax.all_to_all(outbox, 'pool', split_axis=0, concat_axis=0, tiled=True)  7.48 us
    slice x1, local copies, waits for them, and re-layouts, turn_queries(): latent = by_head(query_rows[..., :LATENT_WIDTH])  5.77 us
    all_to_all x2, local copies, waits for them, and re-layouts, shards(): lax.all_to_all(outbox, 'pool', split_axis=0, concat_axis=0, tiled=True)  4.77 us
    gather x1, local copies, waits for them, and re-layouts, shards(): cached_pages = arrived[source]  4.51 us
  transfers between devices with their start and end apart: 1, of which 1 were waited for; matrix products, arithmetic and copies ran while one was open for 20% of the time, Pallas kernels for 0%

profile of v3, /device:TPU:1, one launch (start us, length us, event | category | flops | bytes accessed | tf_op | source)
XLA Modules:
  0.0 180.5 jit_solution(75698510616092119)
XLA Ops:
  0.6 0.0 copy-start
  0.6 0.9 fusion.23
  1.6 0.2 reduce_window_sum.22
  1.8 0.9 select_reduce_fusion
  2.6 0.1 copy.20
  2.7 0.1 reshape.320
  2.8 0.0 copy-done
  2.9 1.6 gather_fusion
  4.5 1.9 %all_to_all.8 = bf16[16,6,9216]{2,1,0:T(8,128)(2,1)} reshape(bf16[96,9216]{1,0:T(8,128)(2,1)S(1)} %gather_fusion) | data formatting | bytes 3538944 | tf_op jit(solution)/shard_map/all_to_all | solution.py:370
  6.4 7.5 %all-to-all-start = ((bf16[16,6,9216]{2,1,0:T(8,128)(2,1)}), bf16[16,6,9216]{2,1,0:T(8,128)(2,1)}, u32[]{:S(2)}, u32[]{:S(2)}) async-start(bf16[16,6,9216]{2,1,0:T(8,128)(2,1)} %all_to_all.8), calls=%async_computation | async-start | bytes 4718592 | tf_op jit(solution)/shard_map/all_to_all | solution.py:370
  13.9 0.0 copy-done.5
  13.9 0.6 dynamic_slice.12
  14.5 0.7 fusion.20
  15.8 0.7 iota_compare_fusion.8
  16.5 0.0 copy-done.9
  16.5 0.6 dynamic_slice.14
  17.1 0.1 broadcast_compare_fusion.1
  17.2 0.0 copy-done.7
  17.2 0.1 fusion.22
  17.3 0.2 reduce_window_sum.23
  17.5 0.1 select_reduce_fusion.1
  17.7 11.5 %reshape.326 = bf16[16,64,4,576]{3,2,1,0:T(4,128)(2,1)} reshape(bf16[1,1024,2304]{2,1,0:T(8,128)(2,1)} %param.9) | data formatting | bytes 9437184 | tf_op jit(solution)/shard_map/reshape | solution.py:400
  29.2 5.8 %slice.48 = bf16[16,64,4,512]{3,2,1,0:T(4,128)(2,1)} slice(bf16[16,64,4,576]{3,2,1,0:T(4,128)(2,1)} %reshape.326), slice={[0:16], [0:64], [0:4], [0:512]} | slice | bytes 8388608 | tf_op jit(solution)/shard_map/slice | solution.py:69
  35.0 0.1 add.167
  35.1 0.1 copy.25
  35.2 0.1 copy.26
  35.3 0.1 broadcast_in_dim.55
  35.4 0.3 broadcast_in_dim.96
  35.7 0.1 reshape.331
  35.8 0.1 add.164
  35.9 0.3 add.170
  36.2 0.0 slice-start
  36.2 5.5 %copy.30 = bf16[16,64,4,512]{3,1,2,0:T(8,128)(2,1)} copy(bf16[16,64,4,512]{3,2,1,0:T(4,128)(2,1)} %slice.48) | data formatting | bytes 8388608
  41.7 0.6 iota_compare_fusion.7
  42.4 0.2 convert_reduce_fusion
  42.5 1.4 fusion.19
  43.9 0.1 multiply_reduce_fusion
  44.0 0.1 add_convert_fusion.1
  44.1 1.9 %multiply_cosine_fusion = (f32[16,64,32]{2,1,0:T(8,128)S(1)}, f32[16,64,32]{2,1,0:T(8,128)S(1)}) fusion(f32[32]{0:T(128)S(1)} %multiply_power_fusion, f32[16,64]{1,0:T(8,128)S(1)} %add_convert_fusion.1), kind=kLoop, calls=%fused_computation.16 | loop fusion | flops 32768 | bytes 266368 | tf_op jit(solution)/shard_map/cos | solution.py:27
  46.0 0.0 slice-done
  46.0 0.3 copy_convert_fusion
  46.3 0.9 subtract_convert_fusion
  47.2 0.6 pad_maximum_fusion
  47.8 0.2 fusion.13
  48.0 0.1 multiply_multiply_fusion
  48.1 0.7 fusion.7
  48.8 1.9 %fusion.2.pq = bf16[16,512,128]{2,1,0:T(8,128)(2,1)} fusion(bf16[16,256,64]{2,1,0:T(8,128)(2,1)S(1)} %bitcast.34), kind=kLoop, calls=%fused_computation.6 | loop fusion | flops 8388608 | bytes 2621440 | tf_op jit(solution)/shard_map/concatenate | solution.py:72
  50.7 0.1 add_select_fusion.rows_sel
  50.8 9.2 %all-to-all-done = bf16[16,6,9216]{2,1,0:T(8,128)(2,1)} async-done(((bf16[16,6,9216]{2,1,0:T(8,128)(2,1)}), bf16[16,6,9216]{2,1,0:T(8,128)(2,1)}, u32[]{:S(2)}, u32[]{:S(2)}) %all-to-all-start) | async-done | bytes 1769504 | tf_op jit(solution)/shard_map/all_to_all | solution.py:370
  60.0 2.9 %all_to_all.10 = bf16[96,9216]{1,0:T(8,128)(2,1)} reshape(bf16[16,6,9216]{2,1,0:T(8,128)(2,1)} %all-to-all-done) | data formatting | bytes 3538944 | tf_op jit(solution)/shard_map/all_to_all | solution.py:370
  62.9 4.5 %gather_fusion.1 = bf16[48,9216]{1,0:T(8,128)(2,1)} fusion(bf16[96,9216]{1,0:T(8,128)(2,1)} %all_to_all.10, s32[1024]{0:T(1024)S(1)} %pad_clamp_fusion), kind=kCustom, calls=%fused_computation.1 | custom fusion | bytes 1769664 | tf_op jit(solution)/shard_map/gather | solution.py:383
  67.4 2.0 %reshape.321 = bf16[768,576]{1,0:T(8,128)(2,1)S(1)} reshape(bf16[48,9216]{1,0:T(8,128)(2,1)} %gather_fusion.1) | data formatting | bytes 1769472 | tf_op jit(solution)/shard_map/reshape | solution.py:394
  69.4 0.8 fusion.6
  70.2 1.8 %fusion.3 = bf16[832,512]{1,0:T(8,128)(2,1)} fusion(bf16[768,576]{1,0:T(8,128)(2,1)S(1)} %reshape.321, bf16[64,576]{1,0:T(8,128)(2,1)} %fusion.7), kind=kLoop, calls=%fused_computation.14 | loop fusion | flops 1703936 | bytes 1810432 | tf_op jit(solution)/shard_map/concatenate | solution.py:394
  72.0 0.1 copy.21
  72.1 0.1 copy.22
  72.3 1.2 pad_maximum_fusion.1.own
  73.5 2.2 %copy-done.1 = bf16[16,64,4,512]{3,1,2,0:T(8,128)(2,1)S(1)} copy-done((bf16[16,64,4,512]{3,1,2,0:T(8,128)(2,1)S(1)}, bf16[16,64,4,512]{3,1,2,0:T(8,128)(2,1)}, u32[]{:S(2)}) %copy-start.1) | copy-done | bytes 4194328
  75.7 1.6 copy-done.2
  77.3 92.3 %shard_map.104 = (bf16[1024,2048]{1,0:T(8,128)(2,1)S(1)}, bf16[16,64,576]{2,1,0:T(8,128)(2,1)S(1)}) custom-call(s32[16]{0:T(128)S(1)} %copy-done.5, s32[16]{0:T(128)S(1)} %get-tuple-element.18.misses, bf16[960,512]{1,0:T(8,128)(2,1)S(1)} %pad_maximum_fusion.1.own, bf16[16,256,512]{2,1,0:T(8,128)(2,1)S(1)} %bitcast.32, bf16[16,512,128]{2,1,0:T(8,128)(2,1)S(1)} %copy-done.2, ...), custom_call_target="tpu_custom_call" | custom-call | tf_op jit(solution)/shard_map/pallas_call | solution.py:320
  169.6 1.9 %copy-done.3 = bf16[1024,2048]{1,0:T(8,128)(2,1)} copy-done((bf16[1024,2048]{1,0:T(8,128)(2,1)}, bf16[1024,2048]{1,0:T(8,128)(2,1)S(1)}, u32[]{:S(2)}) %copy-start.3) | copy-done | bytes 4194328
  171.5 1.1 copy-done.4
  172.6 3.1 %reshape.329 = bf16[64,9216]{1,0:T(8,128)(2,1)} reshape(bf16[16,64,576]{2,1,0:T(8,128)(2,1)} %copy-done.4) | data formatting | bytes 2359296 | tf_op jit(solution)/shard_map/reshape | solution.py:423
  175.7 4.8 %copy.36 = bf16[1,1024,2048]{2,1,0:T(8,128)(2,1)} copy(bf16[1,1024,2048]{2,1,0:T(8,128)(2,1)} %bitcast.33) | data formatting | bytes 8388608
  (27 shorter events, 0.1 us)
Async XLA Ops:
  0.6 2.2 %copy-start = (bf16[96,9216]{1,0:T(8,128)(2,1)S(1)}, bf16[96,9216]{1,0:T(8,128)(2,1)}, u32[]{:S(2)}) copy-start(bf16[96,9216]{1,0:T(8,128)(2,1)} %param.10) | copy-start | bytes 5308420
  6.4 7.5 %copy-start.5 = (s32[16]{0:T(128)S(1)}, s32[16]{0:T(128)}, u32[]{:S(2)}) copy-start(s32[16]{0:T(128)} %hits) | copy-start | bytes 196
  6.4 10.1 %copy-start.9 = (s32[16]{0:T(128)S(1)}, s32[16]{0:T(128)}, u32[]{:S(2)}) copy-start(s32[16]{0:T(128)} %param.14) | copy-start | bytes 196
  6.4 10.8 %copy-start.7 = (s32[16,52,1]{1,2,0:T(1,128)S(1)}, s32[16,52,1]{1,2,0:T(1,128)}, u32[]{:S(2)}) copy-start(s32[16,52,1]{1,2,0:T(1,128)} %param.17) | copy-start | bytes 9988
  6.4 53.6 %all-to-all-start = ((bf16[16,6,9216]{2,1,0:T(8,128)(2,1)}), bf16[16,6,9216]{2,1,0:T(8,128)(2,1)}, u32[]{:S(2)}, u32[]{:S(2)}) async-start(bf16[16,6,9216]{2,1,0:T(8,128)(2,1)} %all_to_all.8), calls=%async_computation | async-start | bytes 4718592 | tf_op jit(solution)/shard_map/all_to_all | solution.py:370
  29.2 5.8 %copy-start.8 = (bf16[512]{0:T(512)(128)(2,1)S(1)}, bf16[512]{0:T(512)(128)(2,1)}, u32[]{:S(2)}) copy-start(bf16[512]{0:T(512)(128)(2,1)} %param.12) | copy-start | bytes 3076
  29.2 6.5 %copy-start.6 = (bf16[4,9216]{1,0:T(4,128)(2,1)S(1)}, bf16[4,9216]{1,0:T(4,128)(2,1)}, u32[]{:S(2)}) copy-start(bf16[4,9216]{1,0:T(4,128)(2,1)} %param.11) | copy-start | bytes 221188
  36.2 9.8 %slice-start = ((bf16[16,64,4,576]{3,2,1,0:T(4,128)(2,1)}), bf16[16,64,4,64]{3,2,1,0:T(4,128)(2,1)S(1)}, s32[]{:S(2)}) async-start(bf16[16,64,4,576]{3,2,1,0:T(4,128)(2,1)} %reshape.326), calls=%async_computation.1 | async-start | bytes 2097152 | tf_op jit(solution)/shard_map/slice | solution.py:65
  73.5 2.2 %copy-start.1 = (bf16[16,64,4,512]{3,1,2,0:T(8,128)(2,1)S(1)}, bf16[16,64,4,512]{3,1,2,0:T(8,128)(2,1)}, u32[]{:S(2)}) copy-start(bf16[16,64,4,512]{3,1,2,0:T(8,128)(2,1)} %copy.30) | copy-start | bytes 12582916
  75.7 1.6 copy-start.2
  169.6 1.9 %copy-start.3 = (bf16[1024,2048]{1,0:T(8,128)(2,1)}, bf16[1024,2048]{1,0:T(8,128)(2,1)S(1)}, u32[]{:S(2)}) copy-start(bf16[1024,2048]{1,0:T(8,128)(2,1)S(1)} %get-tuple-element.4) | copy-start | bytes 12582916
  171.5 1.1 copy-start.4

commit v4 on v3

--- a/solution.py
+++ b/solution.py
@@ -119,9 +119,10 @@
 
 
 def serve_body(
-    key_count, miss_rows, hits, misses, own, lq, pq, rows_sel, context, pages, keys, *sems
+    key_count, miss_rows, hits, misses, own, lq, pq, rows_sel, context, pages, keys, *scratch
 ):
-    local_sem, up_sem, down_sem, y_sem, core_sem, extra_sem, half_sem, recv_sem = sems
+    lq_now, pq_now, context_now, lq_sem, pq_sem, context_sem = scratch[:6]
+    local_sem, up_sem, down_sem, y_sem, core_sem, extra_sem, half_sem, recv_sem = scratch[6:]
     me = lax.axis_index("pool")
     member = lax.rem(me, TPW)
     base = me - member
@@ -226,14 +227,24 @@
 
     def work(slot):
         block = keys.at[slot]
+        fetched = (
+            pltpu.make_async_copy(lq.at[slot], lq_now, lq_sem),
+            pltpu.make_async_copy(pq.at[slot], pq_now, pq_sem),
+        )
+        for item in fetched:
+            item.start()
+        for item in fetched:
+            item.wait()
         result = attend_one(
-            lq[slot], pq[slot], block, hits[slot], misses[slot], key_count, miss_rows
+            lq_now[...], pq_now[...], block, hits[slot], misses[slot], key_count, miss_rows
         ).astype(context.dtype)
         place = pl.ds(pl.multiple_of(slot * miss_rows, miss_rows), miss_rows)
         for head in range(result.shape[0] // miss_rows):
-            context[place, head * LATENT_WIDTH : (head + 1) * LATENT_WIDTH] = result[
+            context_now[:, head * LATENT_WIDTH : (head + 1) * LATENT_WIDTH] = result[
                 head * miss_rows : (head + 1) * miss_rows
             ]
+        stored = pltpu.make_async_copy(context_now, context.at[place], context_sem)
+        stored.start()
         wide = -(-key_count // PACK) * PACK
         chosen = rows_sel[slot] == lax.broadcasted_iota(
             jnp.int32, (rows_sel.shape[1], wide), 1
@@ -253,6 +264,7 @@
         rotary = sums[0][:, :ROPE] + sums[1][:, ROPE:]
         pages[slot, :, :LATENT_WIDTH] = latent.astype(pages.dtype)
         pages[slot, :, LATENT_WIDTH:] = rotary.astype(pages.dtype)
+        stored.wait()
 
     def place_of(distance, way):
         zz = z + jnp.where(way == 0, -distance, distance)
@@ -317,16 +329,23 @@
     picked = jnp.where(picks[:, :, None] >= 0, picked, -1).reshape(prompts, -1, 1)
     vmem = pl.BlockSpec(memory_space=pltpu.VMEM)
     smem = pl.BlockSpec(memory_space=pltpu.SMEM)
+    away = pl.BlockSpec(memory_space=pl.ANY)
     return pl.pallas_call(
         functools.partial(serve_body, key_count, miss_rows),
         out_shape=[
             jax.ShapeDtypeStruct((prompts * miss_rows, heads * LATENT_WIDTH), jnp.bfloat16),
             jax.ShapeDtypeStruct((prompts, picked.shape[1], LATENT_WIDTH + ROPE), jnp.bfloat16),
         ],
-        in_specs=[smem, smem, vmem, vmem, vmem, vmem],
-        out_specs=[vmem, vmem],
+        in_specs=[smem, smem, away, away, away, vmem],
+        out_specs=[away, vmem],
         scratch_shapes=[
             pltpu.VMEM((TPW,) + own.shape, own.dtype),
+            pltpu.VMEM(latent_queries.shape[1:], own.dtype),
+            pltpu.VMEM(paired_queries.shape[1:], own.dtype),
+            pltpu.VMEM((miss_rows, heads * LATENT_WIDTH), jnp.bfloat16),
+            pltpu.SemaphoreType.DMA,
+            pltpu.SemaphoreType.DMA,
+            pltpu.SemaphoreType.DMA,
             pltpu.SemaphoreType.DMA,
             pltpu.SemaphoreType.DMA((4,)),
             pltpu.SemaphoreType.DMA((4,)),
@@ -337,7 +356,7 @@
             pltpu.SemaphoreType.DMA((TPW,)),
         ],
         compiler_params=pltpu.CompilerParams(
-            collective_id=0, has_side_effects=True, vmem_limit_bytes=36 * 1024 * 1024
+            collective_id=0, has_side_effects=True, vmem_limit_bytes=24 * 1024 * 1024
         ),
     )(hits, misses, own, latent_queries, paired_queries, picked)
 

time: 181 us -> 182 us (level)
  no operation moved by 1% of the time
where the time goes in v4:
time: 182 us; the launch traced here: 181 us
  Pallas kernels  92.7 us (51%)
  local copies, waits for them, and re-layouts  53.9 us (30%)
  other arithmetic  16 us (9%)
  waiting for transfers between devices  9.16 us (5%)
  starting transfers between devices  7.48 us (4%)
    pallas_call x1, Pallas kernels, serve(): pl.pallas_call(functools.partial(serve_body, key_count, miss_rows), out_s...  92.7 us
    unnamed x22, local copies, waits for them, and re-layouts  17.1 us
    reshape x1, local copies, waits for them, and re-layouts, shards(): query_rows = queries.reshape(TPW, -1, head_dev, features)  11.5 us
    all_to_all x1, waiting for transfers between devices, shards(): lax.all_to_all(outbox, 'pool', split_axis=0, concat_axis=0, tiled=True)  9.16 us
    all_to_all x1, starting transfers between devices, shards(): lax.all_to_all(outbox, 'pool', split_axis=0, concat_axis=0, tiled=True)  7.48 us
    slice x1, local copies, waits for them, and re-layouts, turn_queries(): latent = by_head(query_rows[..., :LATENT_WIDTH])  5.77 us
    all_to_all x2, local copies, waits for them, and re-layouts, shards(): lax.all_to_all(outbox, 'pool', split_axis=0, concat_axis=0, tiled=True)  4.77 us
    gather x1, local copies, waits for them, and re-layouts, shards(): cached_pages = arrived[source]  4.51 us
  transfers between devices with their start and end apart: 1, of which 1 were waited for; matrix products, arithmetic and copies ran while one was open for 20% of the time, Pallas kernels for 0%

profile of v4, /device:TPU:1, one launch (start us, length us, event | category | flops | bytes accessed | tf_op | source)
XLA Modules:
  0.0 180.9 jit_solution(10093541619890318613)
XLA Ops:
  0.6 0.0 copy-start
  0.6 0.9 fusion.23
  1.6 0.2 reduce_window_sum.22
  1.8 0.9 select_reduce_fusion
  2.6 0.1 copy.20
  2.7 0.1 reshape.320
  2.8 0.0 copy-done
  2.9 1.7 gather_fusion
  4.5 1.9 %all_to_all.8 = bf16[16,6,9216]{2,1,0:T(8,128)(2,1)} reshape(bf16[96,9216]{1,0:T(8,128)(2,1)S(1)} %gather_fusion) | data formatting | bytes 3538944 | tf_op jit(solution)/shard_map/all_to_all | solution.py:389
  6.4 7.5 %all-to-all-start = ((bf16[16,6,9216]{2,1,0:T(8,128)(2,1)}), bf16[16,6,9216]{2,1,0:T(8,128)(2,1)}, u32[]{:S(2)}, u32[]{:S(2)}) async-start(bf16[16,6,9216]{2,1,0:T(8,128)(2,1)} %all_to_all.8), calls=%async_computation | async-start | bytes 4718592 | tf_op jit(solution)/shard_map/all_to_all | solution.py:389
  13.9 0.0 copy-done.5
  13.9 0.6 dynamic_slice.12
  14.5 0.7 fusion.20
  15.8 0.7 iota_compare_fusion.8
  16.5 0.0 copy-done.9
  16.5 0.6 dynamic_slice.14
  17.1 0.1 broadcast_compare_fusion.1
  17.2 0.0 copy-done.7
  17.2 0.1 fusion.22
  17.3 0.2 reduce_window_sum.23
  17.5 0.1 select_reduce_fusion.1
  17.7 11.5 %reshape.326 = bf16[16,64,4,576]{3,2,1,0:T(4,128)(2,1)} reshape(bf16[1,1024,2304]{2,1,0:T(8,128)(2,1)} %param.9) | data formatting | bytes 9437184 | tf_op jit(solution)/shard_map/reshape | solution.py:419
  29.2 5.8 %slice.48 = bf16[16,64,4,512]{3,2,1,0:T(4,128)(2,1)} slice(bf16[16,64,4,576]{3,2,1,0:T(4,128)(2,1)} %reshape.326), slice={[0:16], [0:64], [0:4], [0:512]} | slice | bytes 8388608 | tf_op jit(solution)/shard_map/slice | solution.py:69
  35.0 0.0 copy-done.8
  35.0 0.1 add.167
  35.1 0.1 copy.25
  35.2 0.1 copy.26
  35.3 0.1 broadcast_in_dim.55
  35.4 0.3 broadcast_in_dim.96
  35.7 0.1 reshape.331
  35.8 0.1 add.164
  35.9 0.3 add.170
  36.2 0.0 slice-start
  36.2 5.5 %copy.30 = bf16[16,64,4,512]{3,1,2,0:T(8,128)(2,1)} copy(bf16[16,64,4,512]{3,2,1,0:T(4,128)(2,1)} %slice.48) | data formatting | bytes 8388608
  41.7 0.6 iota_compare_fusion.7
  42.4 0.2 convert_reduce_fusion
  42.5 1.4 fusion.19
  43.9 0.1 multiply_reduce_fusion
  44.0 0.1 add_convert_fusion.1
  44.1 1.9 %multiply_cosine_fusion = (f32[16,64,32]{2,1,0:T(8,128)S(1)}, f32[16,64,32]{2,1,0:T(8,128)S(1)}) fusion(f32[32]{0:T(128)S(1)} %multiply_power_fusion, f32[16,64]{1,0:T(8,128)S(1)} %add_convert_fusion.1), kind=kLoop, calls=%fused_computation.16 | loop fusion | flops 32768 | bytes 266368 | tf_op jit(solution)/shard_map/cos | solution.py:27
  46.0 0.3 copy_convert_fusion
  46.3 0.9 subtract_convert_fusion
  47.2 0.6 pad_maximum_fusion
  47.8 0.2 fusion.13
  48.0 0.1 multiply_multiply_fusion
  48.1 0.7 fusion.7
  48.8 1.9 %fusion.2.pq = bf16[16,512,128]{2,1,0:T(8,128)(2,1)} fusion(bf16[16,256,64]{2,1,0:T(8,128)(2,1)S(1)} %bitcast.34), kind=kLoop, calls=%fused_computation.6 | loop fusion | flops 8388608 | bytes 2621440 | tf_op jit(solution)/shard_map/concatenate | solution.py:72
  50.7 0.1 add_select_fusion.rows_sel
  50.8 9.2 %all-to-all-done = bf16[16,6,9216]{2,1,0:T(8,128)(2,1)} async-done(((bf16[16,6,9216]{2,1,0:T(8,128)(2,1)}), bf16[16,6,9216]{2,1,0:T(8,128)(2,1)}, u32[]{:S(2)}, u32[]{:S(2)}) %all-to-all-start) | async-done | bytes 1769504 | tf_op jit(solution)/shard_map/all_to_all | solution.py:389
  60.0 2.9 %all_to_all.10 = bf16[96,9216]{1,0:T(8,128)(2,1)} reshape(bf16[16,6,9216]{2,1,0:T(8,128)(2,1)} %all-to-all-done) | data formatting | bytes 3538944 | tf_op jit(solution)/shard_map/all_to_all | solution.py:389
  62.9 4.5 %gather_fusion.1 = bf16[48,9216]{1,0:T(8,128)(2,1)} fusion(bf16[96,9216]{1,0:T(8,128)(2,1)} %all_to_all.10, s32[1024]{0:T(1024)S(1)} %pad_clamp_fusion), kind=kCustom, calls=%fused_computation.1 | custom fusion | bytes 1769664 | tf_op jit(solution)/shard_map/gather | solution.py:402
  67.4 2.0 %reshape.321 = bf16[768,576]{1,0:T(8,128)(2,1)S(1)} reshape(bf16[48,9216]{1,0:T(8,128)(2,1)} %gather_fusion.1) | data formatting | bytes 1769472 | tf_op jit(solution)/shard_map/reshape | solution.py:413
  69.4 0.8 fusion.6
  70.2 1.8 fusion.3
  72.0 0.1 copy.21
  72.1 0.1 copy.22
  72.3 1.2 pad_maximum_fusion.1.own
  73.5 2.2 %copy-done.1 = bf16[16,64,4,512]{3,1,2,0:T(8,128)(2,1)S(1)} copy-done((bf16[16,64,4,512]{3,1,2,0:T(8,128)(2,1)S(1)}, bf16[16,64,4,512]{3,1,2,0:T(8,128)(2,1)}, u32[]{:S(2)}) %copy-start.1) | copy-done | bytes 4194328
  75.7 1.6 copy-done.2
  77.3 92.7 %shard_map.104 = (bf16[1024,2048]{1,0:T(8,128)(2,1)S(1)}, bf16[16,64,576]{2,1,0:T(8,128)(2,1)S(1)}) custom-call(s32[16]{0:T(128)S(1)} %copy-done.5, s32[16]{0:T(128)S(1)} %get-tuple-element.18.misses, bf16[960,512]{1,0:T(8,128)(2,1)S(1)} %pad_maximum_fusion.1.own, bf16[16,256,512]{2,1,0:T(8,128)(2,1)S(1)} %bitcast.32, bf16[16,512,128]{2,1,0:T(8,128)(2,1)S(1)} %copy-done.2, ...), custom_call_target="tpu_custom_call" | custom-call | tf_op jit(solution)/shard_map/pallas_call | solution.py:333
  170.0 1.9 %copy-done.3 = bf16[1024,2048]{1,0:T(8,128)(2,1)} copy-done((bf16[1024,2048]{1,0:T(8,128)(2,1)}, bf16[1024,2048]{1,0:T(8,128)(2,1)S(1)}, u32[]{:S(2)}) %copy-start.3) | copy-done | bytes 4194328
  171.9 1.1 copy-done.4
  173.0 3.1 %reshape.329 = bf16[64,9216]{1,0:T(8,128)(2,1)} reshape(bf16[16,64,576]{2,1,0:T(8,128)(2,1)} %copy-done.4) | data formatting | bytes 2359296 | tf_op jit(solution)/shard_map/reshape | solution.py:442
  176.1 4.8 %copy.36 = bf16[1,1024,2048]{2,1,0:T(8,128)(2,1)} copy(bf16[1,1024,2048]{2,1,0:T(8,128)(2,1)} %bitcast.33) | data formatting | bytes 8388608
  (27 shorter events, 0.1 us)
Async XLA Ops:
  0.6 2.2 %copy-start = (bf16[96,9216]{1,0:T(8,128)(2,1)S(1)}, bf16[96,9216]{1,0:T(8,128)(2,1)}, u32[]{:S(2)}) copy-start(bf16[96,9216]{1,0:T(8,128)(2,1)} %param.10) | copy-start | bytes 5308420
  6.4 7.5 %copy-start.5 = (s32[16]{0:T(128)S(1)}, s32[16]{0:T(128)}, u32[]{:S(2)}) copy-start(s32[16]{0:T(128)} %hits) | copy-start | bytes 196
  6.4 10.1 %copy-start.9 = (s32[16]{0:T(128)S(1)}, s32[16]{0:T(128)}, u32[]{:S(2)}) copy-start(s32[16]{0:T(128)} %param.14) | copy-start | bytes 196
  6.4 10.8 %copy-start.7 = (s32[16,52,1]{1,2,0:T(1,128)S(1)}, s32[16,52,1]{1,2,0:T(1,128)}, u32[]{:S(2)}) copy-start(s32[16,52,1]{1,2,0:T(1,128)} %param.17) | copy-start | bytes 9988
  6.4 53.6 %all-to-all-start = ((bf16[16,6,9216]{2,1,0:T(8,128)(2,1)}), bf16[16,6,9216]{2,1,0:T(8,128)(2,1)}, u32[]{:S(2)}, u32[]{:S(2)}) async-start(bf16[16,6,9216]{2,1,0:T(8,128)(2,1)} %all_to_all.8), calls=%async_computation | async-start | bytes 4718592 | tf_op jit(solution)/shard_map/all_to_all | solution.py:389
  29.2 5.8 %copy-start.8 = (bf16[512]{0:T(512)(128)(2,1)S(1)}, bf16[512]{0:T(512)(128)(2,1)}, u32[]{:S(2)}) copy-start(bf16[512]{0:T(512)(128)(2,1)} %param.12) | copy-start | bytes 3076
  29.2 6.5 %copy-start.6 = (bf16[4,9216]{1,0:T(4,128)(2,1)S(1)}, bf16[4,9216]{1,0:T(4,128)(2,1)}, u32[]{:S(2)}) copy-start(bf16[4,9216]{1,0:T(4,128)(2,1)} %param.11) | copy-start | bytes 221188
  36.2 9.8 %slice-start = ((bf16[16,64,4,576]{3,2,1,0:T(4,128)(2,1)}), bf16[16,64,4,64]{3,2,1,0:T(4,128)(2,1)S(1)}, s32[]{:S(2)}) async-start(bf16[16,64,4,576]{3,2,1,0:T(4,128)(2,1)} %reshape.326), calls=%async_computation.1 | async-start | bytes 2097152 | tf_op jit(solution)/shard_map/slice | solution.py:65
  73.5 2.2 %copy-start.1 = (bf16[16,64,4,512]{3,1,2,0:T(8,128)(2,1)S(1)}, bf16[16,64,4,512]{3,1,2,0:T(8,128)(2,1)}, u32[]{:S(2)}) copy-start(bf16[16,64,4,512]{3,1,2,0:T(8,128)(2,1)} %copy.30) | copy-start | bytes 12582916
  75.7 1.6 copy-start.2
  170.0 1.9 %copy-start.3 = (bf16[1024,2048]{1,0:T(8,128)(2,1)}, bf16[1024,2048]{1,0:T(8,128)(2,1)S(1)}, u32[]{:S(2)}) copy-start(bf16[1024,2048]{1,0:T(8,128)(2,1)S(1)} %get-tuple-element.4) | copy-start | bytes 12582916
  171.9 1.1 copy-start.4

commit v5 on v4

--- a/solution.py
+++ b/solution.py
@@ -356,7 +356,7 @@
             pltpu.SemaphoreType.DMA((TPW,)),
         ],
         compiler_params=pltpu.CompilerParams(
-            collective_id=0, has_side_effects=True, vmem_limit_bytes=24 * 1024 * 1024
+            collective_id=0, has_side_effects=True, vmem_limit_bytes=58 * 1024 * 1024
         ),
     )(hits, misses, own, latent_queries, paired_queries, picked)
 

time: 182 us -> 176 us (0.967)
  local copies, waits for them, and re-layouts: 53.9 us -> 43.8 us
  Pallas kernels: 92.7 us -> 96.1 us
    unnamed x22 -> x18, local copies, waits for them, and re-layouts: 17.1 us -> 10.3 us
    pallas_call x1, Pallas kernels: 92.7 us -> 96.1 us  [serve(): pl.pallas_call(functools.partial(serve_body, key_count, miss_rows), out_s...]
    gather x1, local copies, waits for them, and re-layouts: 4.51 us -> 2.01 us  [shards(): cached_pages = arrived[source]]
  transfers between devices with their start and end apart: 1 -> 1, of which waited for: 1 -> 1; matrix products, arithmetic and copies ran while one was open for 20% -> 21% of each run, Pallas kernels for 0% -> 0%
where the time goes in v5:
time: 176 us; the launch traced here: 174 us
  Pallas kernels  96.1 us (55%)
  local copies, waits for them, and re-layouts  43.8 us (25%)
  other arithmetic  16.9 us (10%)
  waiting for transfers between devices  8.37 us (5%)
  starting transfers between devices  7.48 us (4%)
    pallas_call x1, Pallas kernels, serve(): pl.pallas_call(functools.partial(serve_body, key_count, miss_rows), out_s...  96.1 us
    reshape x1, local copies, waits for them, and re-layouts, shards(): query_rows = queries.reshape(TPW, -1, head_dev, features)  11.5 us
    unnamed x18, local copies, waits for them, and re-layouts  10.3 us
    all_to_all x1, waiting for transfers between devices, shards(): lax.all_to_all(outbox, 'pool', split_axis=0, concat_axis=0, tiled=True)  8.37 us
    all_to_all x1, starting transfers between devices, shards(): lax.all_to_all(outbox, 'pool', split_axis=0, concat_axis=0, tiled=True)  7.48 us
    slice x1, local copies, waits for them, and re-layouts, turn_queries(): latent = by_head(query_rows[..., :LATENT_WIDTH])  5.77 us
    all_to_all x2, local copies, waits for them, and re-layouts, shards(): lax.all_to_all(outbox, 'pool', split_axis=0, concat_axis=0, tiled=True)  3.83 us
  transfers between devices with their start and end apart: 1, of which 1 were waited for; matrix products, arithmetic and copies ran while one was open for 21% of the time, Pallas kernels for 0%

profile of v5, /device:TPU:1, one launch (start us, length us, event | category | flops | bytes accessed | tf_op | source)
XLA Modules:
  0.0 174.3 jit_solution(2334103683277200051)
XLA Ops:
  0.6 0.0 copy-start
  0.6 0.9 fusion.23
  1.6 0.2 reduce_window_sum.22
  1.8 0.9 select_reduce_fusion
  2.6 0.1 copy.20
  2.7 0.1 reshape.320
  2.8 0.0 copy-done
  2.9 1.7 gather_fusion
  4.5 1.9 %all_to_all.8 = bf16[16,6,9216]{2,1,0:T(8,128)(2,1)} reshape(bf16[96,9216]{1,0:T(8,128)(2,1)S(1)} %gather_fusion) | data formatting | bytes 3538944 | tf_op jit(solution)/shard_map/all_to_all | solution.py:389
  6.4 7.5 %all-to-all-start = ((bf16[16,6,9216]{2,1,0:T(8,128)(2,1)}), bf16[16,6,9216]{2,1,0:T(8,128)(2,1)}, u32[]{:S(2)}, u32[]{:S(2)}) async-start(bf16[16,6,9216]{2,1,0:T(8,128)(2,1)} %all_to_all.8), calls=%async_computation | async-start | bytes 4718592 | tf_op jit(solution)/shard_map/all_to_all | solution.py:389
  13.9 0.0 copy-done.4
  13.9 0.6 dynamic_slice.12
  14.5 0.7 fusion.20
  15.8 0.7 iota_compare_fusion.8
  16.5 0.0 copy-done.7
  16.5 0.0 copy-start.5
  16.5 0.6 dynamic_slice.14
  17.2 0.1 broadcast_compare_fusion.1
  17.2 0.0 copy-done.3
  17.3 0.1 fusion.22
  17.3 0.2 reduce_window_sum.23
  17.5 0.1 select_reduce_fusion.1
  17.7 11.5 %reshape.326 = bf16[16,64,4,576]{3,2,1,0:T(4,128)(2,1)} reshape(bf16[1,1024,2304]{2,1,0:T(8,128)(2,1)} %param.9) | data formatting | bytes 9437184 | tf_op jit(solution)/shard_map/reshape | solution.py:419
  29.2 0.0 copy-done.5
  29.2 5.8 %slice.48 = bf16[16,64,4,512]{3,2,1,0:T(4,128)(2,1)} slice(bf16[16,64,4,576]{3,2,1,0:T(4,128)(2,1)} %reshape.326), slice={[0:16], [0:64], [0:4], [0:512]} | slice | bytes 8388608 | tf_op jit(solution)/shard_map/slice | solution.py:69
  35.0 0.0 copy-done.6
  35.0 0.1 add.167
  35.1 0.1 copy.25
  35.2 0.1 copy.26
  35.3 0.1 broadcast_in_dim.55
  35.4 0.3 broadcast_in_dim.96
  35.7 0.0 copy-done.2
  35.7 0.1 reshape.331
  35.9 0.1 add.164
  35.9 0.3 add.170
  36.2 0.0 slice-start
  36.3 5.5 %copy.30 = bf16[16,64,4,512]{3,1,2,0:T(8,128)(2,1)} copy(bf16[16,64,4,512]{3,2,1,0:T(4,128)(2,1)} %slice.48) | data formatting | bytes 8388608
  41.8 0.6 iota_compare_fusion.7
  42.4 0.2 convert_reduce_fusion
  42.6 1.4 fusion.19
  43.9 0.1 multiply_reduce_fusion
  44.0 0.1 add_convert_fusion.1
  44.1 1.9 %multiply_cosine_fusion = (f32[16,64,32]{2,1,0:T(8,128)S(1)}, f32[16,64,32]{2,1,0:T(8,128)S(1)}) fusion(f32[32]{0:T(128)S(1)} %multiply_power_fusion, f32[16,64]{1,0:T(8,128)S(1)} %add_convert_fusion.1), kind=kLoop, calls=%fused_computation.16 | loop fusion | flops 32768 | bytes 266368 | tf_op jit(solution)/shard_map/cos | solution.py:27
  46.0 0.0 slice-done
  46.0 0.3 copy_convert_fusion
  46.3 0.9 subtract_convert_fusion
  47.1 0.6 pad_maximum_fusion
  47.7 0.2 fusion.13
  47.9 0.1 multiply_multiply_fusion
  48.0 0.7 fusion.7
  48.8 1.9 %fusion.2.pq = bf16[16,512,128]{2,1,0:T(8,128)(2,1)} fusion(bf16[16,256,64]{2,1,0:T(8,128)(2,1)S(1)} %bitcast.33), kind=kLoop, calls=%fused_computation.6 | loop fusion | flops 8388608 | bytes 2621440 | tf_op jit(solution)/shard_map/concatenate | solution.py:72
  50.7 1.0 add_select_fusion.rows_sel
  51.6 8.4 %all-to-all-done = bf16[16,6,9216]{2,1,0:T(8,128)(2,1)} async-done(((bf16[16,6,9216]{2,1,0:T(8,128)(2,1)}), bf16[16,6,9216]{2,1,0:T(8,128)(2,1)}, u32[]{:S(2)}, u32[]{:S(2)}) %all-to-all-start) | async-done | bytes 1769504 | tf_op jit(solution)/shard_map/all_to_all | solution.py:389
  60.0 2.0 %all_to_all.10 = bf16[96,9216]{1,0:T(8,128)(2,1)S(1)} reshape(bf16[16,6,9216]{2,1,0:T(8,128)(2,1)} %all-to-all-done) | data formatting | bytes 3538944 | tf_op jit(solution)/shard_map/all_to_all | solution.py:389
  62.0 2.0 %gather_fusion.1 = bf16[48,9216]{1,0:T(8,128)(2,1)} fusion(bf16[96,9216]{1,0:T(8,128)(2,1)S(1)} %all_to_all.10, s32[1024]{0:T(1024)S(1)} %pad_clamp_fusion), kind=kCustom, calls=%fused_computation.1 | custom fusion | bytes 1769664 | tf_op jit(solution)/shard_map/gather | solution.py:402
  64.0 2.0 %reshape.321 = bf16[768,576]{1,0:T(8,128)(2,1)S(1)} reshape(bf16[48,9216]{1,0:T(8,128)(2,1)} %gather_fusion.1) | data formatting | bytes 1769472 | tf_op jit(solution)/shard_map/reshape | solution.py:413
  66.0 0.8 fusion.6
  66.8 1.0 fusion.3
  67.8 0.1 copy.21
  67.9 0.1 copy.22
  68.0 2.2 %pad_maximum_fusion.1.own = bf16[960,512]{1,0:T(8,128)(2,1)} fusion(bf16[128,512]{1,0:T(8,128)(2,1)S(1)} %copy.22, bf16[832,512]{1,0:T(8,128)(2,1)} %fusion.3), kind=kLoop, calls=%fused_computation.13 | loop fusion | flops 1966080 | bytes 1966080 | tf_op jit(solution)/shard_map/concatenate | solution.py:83
  70.2 96.1 %shard_map.104 = (bf16[1024,2048]{1,0:T(8,128)(2,1)}, bf16[16,64,576]{2,1,0:T(8,128)(2,1)}) custom-call(s32[16]{0:T(128)} %hits, s32[16]{0:T(128)} %copy-done.5, bf16[960,512]{1,0:T(8,128)(2,1)} %pad_maximum_fusion.1.own, bf16[16,256,512]{2,1,0:T(8,128)(2,1)} %bitcast.32, bf16[16,512,128]{2,1,0:T(8,128)(2,1)} %fusion.2.pq, s32[16,64,1]{2,1,0:T(8,128)} %add_select_fusion.rows_sel), custom_call_target="tpu_custom_call" | custom-call | tf_op jit(solution)/shard_map/pallas_call | solution.py:333
  166.3 3.1 %reshape.329 = bf16[64,9216]{1,0:T(8,128)(2,1)} reshape(bf16[16,64,576]{2,1,0:T(8,128)(2,1)} %get-tuple-element.5) | data formatting | bytes 2359296 | tf_op jit(solution)/shard_map/reshape | solution.py:442
  169.5 4.8 %copy.36 = bf16[1,1024,2048]{2,1,0:T(8,128)(2,1)} copy(bf16[1,1024,2048]{2,1,0:T(8,128)(2,1)} %bitcast.34) | data formatting | bytes 8388608
  (23 shorter events, 0.1 us)
Async XLA Ops:
  0.6 2.2 %copy-start = (bf16[96,9216]{1,0:T(8,128)(2,1)S(1)}, bf16[96,9216]{1,0:T(8,128)(2,1)}, u32[]{:S(2)}) copy-start(bf16[96,9216]{1,0:T(8,128)(2,1)} %param.10) | copy-start | bytes 5308420
  6.4 7.5 %copy-start.4 = (s32[16]{0:T(128)S(1)}, s32[16]{0:T(128)}, u32[]{:S(2)}) copy-start(s32[16]{0:T(128)} %hits) | copy-start | bytes 196
  6.4 10.1 %copy-start.7 = (s32[16]{0:T(128)S(1)}, s32[16]{0:T(128)}, u32[]{:S(2)}) copy-start(s32[16]{0:T(128)} %param.14) | copy-start | bytes 196
  6.4 10.9 %copy-start.3 = (s32[16,52,1]{1,2,0:T(1,128)S(1)}, s32[16,52,1]{1,2,0:T(1,128)}, u32[]{:S(2)}) copy-start(s32[16,52,1]{1,2,0:T(1,128)} %param.17) | copy-start | bytes 9988
  6.4 53.6 %all-to-all-start = ((bf16[16,6,9216]{2,1,0:T(8,128)(2,1)}), bf16[16,6,9216]{2,1,0:T(8,128)(2,1)}, u32[]{:S(2)}, u32[]{:S(2)}) async-start(bf16[16,6,9216]{2,1,0:T(8,128)(2,1)} %all_to_all.8), calls=%async_computation | async-start | bytes 4718592 | tf_op jit(solution)/shard_map/all_to_all | solution.py:389
  16.5 12.7 %copy-start.5 = (s32[16]{0:T(128)}, s32[16]{0:T(128)S(1)}, u32[]{:S(2)}) copy-start(s32[16]{0:T(128)S(1)} %get-tuple-element.18.misses) | copy-start | bytes 196
  29.2 5.8 %copy-start.6 = (bf16[512]{0:T(512)(128)(2,1)S(1)}, bf16[512]{0:T(512)(128)(2,1)}, u32[]{:S(2)}) copy-start(bf16[512]{0:T(512)(128)(2,1)} %param.12) | copy-start | bytes 3076
  29.2 6.5 %copy-start.2 = (bf16[4,9216]{1,0:T(4,128)(2,1)S(1)}, bf16[4,9216]{1,0:T(4,128)(2,1)}, u32[]{:S(2)}) copy-start(bf16[4,9216]{1,0:T(4,128)(2,1)} %param.11) | copy-start | bytes 221188
  36.2 9.8 %slice-start = ((bf16[16,64,4,576]{3,2,1,0:T(4,128)(2,1)}), bf16[16,64,4,64]{3,2,1,0:T(4,128)(2,1)S(1)}, s32[]{:S(2)}) async-start(bf16[16,64,4,576]{3,2,1,0:T(4,128)(2,1)} %reshape.326), calls=%async_computation.1 | async-start | bytes 2097152 | tf_op jit(solution)/shard_map/slice | solution.py:65
  64.0 2.8 %copy-start.1 = (bf16[64,576]{1,0:T(8,128)(2,1)S(1)}, bf16[64,576]{1,0:T(8,128)(2,1)}, u32[]{:S(2)}) copy-start(bf16[64,576]{1,0:T(8,128)(2,1)} %fusion.7) | copy-start | bytes 221188
